TPU v7x, 32 devices: a whole 2x2x4 slice. The times are simulated.
32 devices in a mesh: body: 2 (over core), gx: 4 (over y, x), gy: 4 (over z).
Axes of the slice: x: 2, y: 2, z: 4, core: 2. Of those that a mesh axis runs over, the one named last changes fastest.
Arguments:
- surface_disp: float32 [2, 3, 49, 8192], P('body', None, None, ('gx', 'gy')), may hold values from -6 to 6
- proj_coords: float32 [2, 2, 36, 4096], P('body', None, None, ('gx', 'gy')), may hold values from -1 to 1
- pair_slave: int32 [2, 4096], P('body', ('gx', 'gy')), may hold values from 0 to 511
- pair_owner: int32 [2, 4096, 1], P('body', ('gx', 'gy')), may hold values from 0 to 15; in each aligned block of 256 rows (0 to 255, 256 to 511, ..., all dimensions but the last counted through in order) at most 24 rows name the same one
- send_list: int32 [2, 16, 384], P(None, ('gx', 'gy')), may hold values from 0 to 511
Outputs:
- nodal_force: float32 [2, 3, 192, 1536], P('body', None, 'gx', 'gy')
Inputs may be any that keep to these rules, and one draw needn't show every extreme that they name: `pair_owner`: within the 256 pairs of one slave tile, at most 24 name the same owner tile; in some tile exactly 24 do.
All inputs are finite; a program needn't handle non-finite values.
Results may differ from a plain program's by a relative error of at most 0.0003.
Values sent between devices are 32-bit elements; how exact they have to be, the bound alone decides.
A program may use at most 64 MiB of HBM per device.

v0:
```python
import jax
import jax.numpy as jnp
from jax import lax
from jax.sharding import PartitionSpec as P

SX = 8
SY = 64


KAPPA = 2.0
SHEAR = 1.0
LOBATTO_POINTS = (
    -1.0,
    -0.830223896278567,
    -0.4688487934707142,
    0.0,
    0.4688487934707142,
    0.830223896278567,
    1.0,
)
GAUSS_POINTS = (
    -0.932469514203152,
    -0.6612093864662645,
    -0.2386191860831969,
    0.2386191860831969,
    0.6612093864662645,
    0.932469514203152,
)
GAUSS_WEIGHTS = (
    0.1713244923791704,
    0.3607615730481386,
    0.467913934572691,
    0.467913934572691,
    0.3607615730481386,
    0.1713244923791704,
)


def from_partner(value, axis, bit):
    return lax.ppermute(value, axis, [(i, i ^ 1 << bit) for i in range(lax.axis_size(axis))])


def from_behind(value, axis, by):
    length = lax.axis_size(axis)
    return lax.ppermute(value, axis, [(i, (i + by) % length) for i in range(length)])


def basis_traced(abscissa):
    points = LOBATTO_POINTS
    factors = []
    for k in range(7):
        product = jnp.ones_like(abscissa)
        for m in range(7):
            if m != k:
                product = product * ((abscissa - points[m]) * (1.0 / (points[k] - points[m])))
        factors.append(product)
    return jnp.stack(factors)


def slave_table():
    single = basis_traced(jnp.asarray(GAUSS_POINTS, jnp.float32)).T
    return (single[:, None, :, None] * single[None, :, None, :]).reshape(36, 49)


def quad_weights():
    weights = jnp.asarray(GAUSS_WEIGHTS, jnp.float32)
    return (weights[:, None] * weights[None, :]).reshape(36)


def pair_forces(slave_nodes, master_nodes, pair_coords, normal_sign):
    highest = lax.Precision.HIGHEST
    slave_basis = slave_table()
    quad_weight = quad_weights()
    first_basis = basis_traced(pair_coords[0])
    second_basis = basis_traced(pair_coords[1])
    slave_value = jnp.einsum("qi,cip->cqp", slave_basis, slave_nodes, precision=highest)
    master_grid = master_nodes.reshape(3, 7, 7, -1)
    partial_sum = jnp.einsum("lqp,cklp->ckqp", second_basis, master_grid, precision=highest)
    master_value = jnp.sum(first_basis[None] * partial_sum, axis=1)
    offset = master_value - slave_value
    normal_gap = normal_sign * offset[2]
    pressure = KAPPA * jax.nn.softplus(-normal_gap)
    traction = (
        jnp.stack([SHEAR * offset[0], SHEAR * offset[1], -normal_sign * pressure])
        * quad_weight[None, :, None]
    )
    slave_force = jnp.einsum("qi,cqp->cip", slave_basis, traction, precision=highest)
    weighted = second_basis[None] * traction[:, None]
    master_force = -jnp.einsum("kqp,clqp->cklp", first_basis, weighted, precision=highest).reshape(
        3, 49, -1
    )
    return (slave_force, master_force)


def slot_ranks(owners, tile_count):
    onehot = (owners[:, None] == jnp.arange(tile_count, dtype=jnp.int32)[None, :]).astype(jnp.int32)
    before = jnp.cumsum(onehot, axis=0) - onehot
    return jnp.sum(before * onehot, axis=1)


def cross_body(payload):
    return from_partner(payload, "body", 0)


def across_tiles(buffer):
    return lax.all_to_all(
        lax.all_to_all(buffer, "gx", split_axis=2, concat_axis=2, tiled=True),
        "gy",
        split_axis=3,
        concat_axis=3,
        tiled=True,
    )


def assemble_local(element_force, seg_x, seg_y):
    segment_grid = element_force.reshape(3, 7, 7, seg_x, seg_y)
    rim_x = from_behind(segment_grid[:, 6, :, seg_x - 1 :, :], "gx", 1)
    incoming_x = jnp.concatenate([rim_x, segment_grid[:, 6, :, : seg_x - 1, :]], axis=2)
    along_x = segment_grid[:, :6].at[:, 0].add(incoming_x)
    rim_y = from_behind(along_x[:, :, 6, :, seg_y - 1 :], "gy", 1)
    incoming_y = jnp.concatenate([rim_y, along_x[:, :, 6, :, : seg_y - 1]], axis=3)
    along_y = along_x[:, :, :6].at[:, :, 0].add(incoming_y)
    return along_y.transpose(0, 3, 1, 4, 2).reshape(3, 6 * seg_x, 6 * seg_y)


def local(surface_disp, proj_coords, pair_slave, pair_owner, send_list):
    width_x = lax.axis_size("gx")
    width_y = lax.axis_size("gy")
    tile_count = width_x * width_y
    body_side = lax.axis_index("body")
    normal_sign = 1.0 - 2.0 * body_side.astype(jnp.float32)
    own_surface = surface_disp[0]
    segment_count = own_surface.shape[-1]
    slots_total = send_list.shape[-1]
    slot_capacity = slots_total // tile_count
    own_list = jnp.where(body_side == 0, send_list[0, 0], send_list[1, 0])
    owners = pair_owner[0, :, 0]
    slot_index = owners * slot_capacity + slot_ranks(owners, tile_count)
    slave_nodes = jnp.take(own_surface, pair_slave[0], axis=2)
    outgoing = jnp.take(own_surface, own_list, axis=2)
    arrived = across_tiles(outgoing.reshape(3, 49, width_x, width_y * slot_capacity))
    received = cross_body(arrived).reshape(3, 49, slots_total)
    master_nodes = jnp.take(received, slot_index, axis=2)
    slave_force, master_force = pair_forces(slave_nodes, master_nodes, proj_coords[0], normal_sign)
    element_force = (
        jnp.zeros((3, 49, segment_count), jnp.float32).at[:, :, pair_slave[0]].add(slave_force)
    )
    slot_force = jnp.zeros((3, 49, slots_total), jnp.float32).at[:, :, slot_index].add(master_force)
    crossed = cross_body(slot_force).reshape(3, 49, width_x, width_y * slot_capacity)
    returned = across_tiles(crossed).reshape(3, 49, slots_total)
    element_force = element_force + jnp.zeros((3, 49, segment_count), jnp.float32).at[
        :, :, own_list
    ].add(returned)
    nodal = assemble_local(element_force, SX, SY)
    return nodal[None]


def solution(mesh):
    return jax.shard_map(
        local,
        mesh=mesh,
        in_specs=(
            P("body", None, None, ("gx", "gy")),
            P("body", None, None, ("gx", "gy")),
            P("body", ("gx", "gy")),
            P("body", ("gx", "gy"), None),
            P(None, ("gx", "gy"), None),
        ),
        out_specs=P("body", None, "gx", "gy"),
        check_vma=False,
    )
```

profile of v0, /device:TPU:0, one launch (start us, length us, event | category | flops | bytes accessed | tf_op | source)
XLA Modules:
  0.0 135.6 jit_solution(9685165475016290781)
XLA Ops:
  1.5 1.4 %copy.76 = f32[1,3,49,512]{2,1,3,0:T(4,128)S(1)} copy(f32[1,3,49,512]{3,0,2,1:T(1,128)} %param.11) | data formatting | bytes 602112 | tf_op args[0]
  2.9 2.0 %gather_fusion = f32[384,3,49]{2,1,0:T(4,128)S(1)} fusion(f32[3,49,512]{1,0,2:T(4,128)S(1)} %bitcast.286, s32[1024]{0:T(1024)S(1)} %get-tuple-element.34), kind=kCustom, calls=%fused_computation | custom fusion | bytes 453120 | tf_op jit(solution)/shard_map/jit(_take)/gather | solution.py:140
  6.0 5.2 %all-to-all-start = ((f32[3,49,4,96]{3,1,0,2:T(8,128)}), f32[3,49,4,96]{3,1,0,2:T(8,128)S(1)}, u32[]{:S(2)}, u32[]{:S(2)}) async-start(f32[3,49,4,96]{3,1,0,2:T(8,128)} %broadcast_select_fusion), calls=%async_computation | async-start | bytes 688128 | tf_op jit(solution)/shard_map/all_to_all | solution.py:107
  12.9 4.4 %all-to-all-done = f32[3,49,4,96]{3,1,0,2:T(8,128)S(1)} async-done(((f32[3,49,4,96]{3,1,0,2:T(8,128)}), f32[3,49,4,96]{3,1,0,2:T(8,128)S(1)}, u32[]{:S(2)}, u32[]{:S(2)}) %all-to-all-start) | async-done | bytes 225824 | tf_op jit(solution)/shard_map/all_to_all | solution.py:107
  17.6 1.5 %reshape.1157 = f32[4,1,14112]{2,1,0:T(1,128)} reshape(f32[96,3,4,49]{3,2,1,0:T(4,128)S(1)} %bitcast.282) | data formatting | bytes 451584
  19.1 4.9 %all-to-all-start.1 = ((f32[4,1,14112]{2,1,0:T(1,128)}), f32[4,1,14112]{2,1,0:T(1,128)S(1)}, u32[]{:S(2)}, u32[]{:S(2)}) async-start(f32[4,1,14112]{2,1,0:T(1,128)} %reshape.1157), calls=%async_computation.1 | async-start | bytes 454656 | tf_op jit(solution)/shard_map/all_to_all | solution.py:106
  25.0 1.1 select_bitcast_fusion
  26.1 4.5 %all-to-all-done.1 = f32[4,1,14112]{2,1,0:T(1,128)S(1)} async-done(((f32[4,1,14112]{2,1,0:T(1,128)}), f32[4,1,14112]{2,1,0:T(1,128)S(1)}, u32[]{:S(2)}, u32[]{:S(2)}) %all-to-all-start.1) | async-done | bytes 225824 | tf_op jit(solution)/shard_map/all_to_all | solution.py:106
  31.1 1.3 reduce.10
  33.6 1.4 %copy.88 = f32[7,36,256]{1,0,2:T(8,128)} copy(f32[7,36,256]{2,1,0:T(8,128)S(1)} %get-tuple-element.35) | data formatting | bytes 516096 | tf_op jit(solution)/shard_map/stack | solution.py:57
  34.9 1.4 copy.101
  36.3 1.3 copy.74
  37.8 1.4 %copy.102 = f32[7,36,256,1]{1,0,3,2:T(8,128)} copy(f32[7,36,256,1]{2,1,0,3:T(8,128)S(1)} %bitcast.291) | data formatting | bytes 516096 | tf_op jit(solution)/shard_map/stack | solution.py:57
  40.9 1.1 copy.83
  42.0 8.7 %fusion = f32[3,36,256]{1,0,2:T(4,128)} fusion(f32[3,7,7,256]{2,1,0,3:T(8,128)S(1)} %copy.83, f32[7,36,256,1]{1,0,3,2:T(8,128)} %copy.101, f32[7,36,256]{1,0,2:T(8,128)} %copy.74), kind=kOutput, calls=%fused_computation.7 | convolution fusion | flops 16616448 | bytes 777216 | tf_op jit(solution)/shard_map/lqp,cklp->ckqp/dot_general | solution.py:78
  50.7 1.2 copy.86
  51.9 1.6 %fusion.7 = f32[3,36,256]{2,1,0:T(8,128)S(1)} fusion(f32[3,36,256]{2,1,0:T(8,128)S(1)} %copy.86, f32[36,49,1]{1,0,2:T(8,128)S(1)} %reshape.1151, f32[3,49,256]{1,0,2:T(4,128)} %select_bitcast_fusion), kind=kOutput, calls=%fused_computation.15 | convolution fusion | flops 16284672 | bytes 378768 | tf_op jit(solution)/shard_map/qi,cip->cqp/dot_general | solution.py:76
  54.6 7.5 %negate_bitcast_fusion = f32[3,7,7,256]{1,2,0,3:T(8,128)S(1)} fusion(f32[7,36,256,1]{1,0,3,2:T(8,128)} %copy.102, f32[3,36,256]{1,0,2:T(4,128)} %copy.89, f32[7,36,256]{1,0,2:T(8,128)} %copy.88), kind=kOutput, calls=%fused_computation.8 | convolution fusion | flops 16488192 | bytes 777216 | tf_op jit(solution)/shard_map/kqp,clqp->cklp/dot_general | solution.py:89
  62.0 1.2 copy.91
  63.6 8.3 %scatter_fusion.1 = f32[3,49,384]{1,0,2:T(4,128)S(1)} fusion(f32[3,49,384]{1,0,2:T(4,128)S(1)} %broadcast_in_dim.50, s32[256]{0:T(256)S(1)} %bitcast.300, f32[256,3,49]{2,1,0:T(4,128)S(1)} %copy.92), kind=kCustom, calls=%fused_computation.4 | custom fusion | flops 37632 | bytes 452608 | tf_op jit(solution)/shard_map/scatter-add | solution.py:148
  72.8 1.2 collective-permute-done.1
  74.2 9.9 %all_to_all.20 = f32[3,49,4,96]{3,1,0,2:T(8,128)S(1)} all-to-all(f32[3,49,4,96]{3,1,0,2:T(8,128)S(1)} %copy.94), channel_id=1, replica_groups=mesh['body'=2,'gx'=4,'gy'=4] {'gx'}, dimensions={2} | all-to-all | bytes 451584 | tf_op jit(solution)/shard_map/all_to_all | solution.py:107
  84.4 1.5 %reshape.1159 = f32[4,1,14112]{2,1,0:T(1,128)} reshape(f32[96,3,4,49]{3,2,1,0:T(4,128)S(1)} %bitcast.283) | data formatting | bytes 451584
  85.9 3.6 %all-to-all-start.3 = ((f32[4,1,14112]{2,1,0:T(1,128)}), f32[4,1,14112]{2,1,0:T(1,128)S(1)}, u32[]{:S(2)}, u32[]{:S(2)}) async-start(f32[4,1,14112]{2,1,0:T(1,128)} %reshape.1159), calls=%async_computation.3 | async-start | bytes 454656 | tf_op jit(solution)/shard_map/all_to_all | solution.py:106
  90.3 8.3 %scatter_fusion = f32[3,49,512]{1,0,2:T(4,128)S(1)} fusion(f32[3,49,512]{1,0,2:T(4,128)S(1)} %broadcast.1275.clone, s32[256]{0:T(256)S(1)} %bitcast.303, f32[256,3,49]{2,1,0:T(4,128)S(1)} %copy.87), kind=kCustom, calls=%fused_computation.3 | custom fusion | flops 37632 | bytes 452608 | tf_op jit(solution)/shard_map/scatter-add | solution.py:146
  98.7 1.3 reduce.11
  101.7 14.2 %scatter_fusion.2 = f32[3,49,512]{1,0,2:T(4,128)S(1)} fusion(f32[3,49,512]{1,0,2:T(4,128)S(1)} %broadcast.1275.clone.1, s32[384]{0:T(512)S(1)} %fusion.29, f32[384,3,49]{2,1,0:T(4,128)S(1)} %copy.97), kind=kCustom, calls=%fused_computation.5 | custom fusion | flops 56448 | bytes 678912 | tf_op jit(solution)/shard_map/scatter-add | solution.py:153
  117.6 3.7 %collective-permute-done.2 = f32[3,7,1,64]{3,2,1,0:T(1,128)S(1)} collective-permute-done((f32[3,7,1,64]{3,2,1,0:T(1,128)S(1)}, f32[3,7,1,64]{3,2,1,0:T(1,128)S(1)}, u32[]{:S(2)}, u32[]{:S(2)}) %collective-permute-start.2) | collective-permute-done | bytes 5408 | tf_op jit(solution)/shard_map/ppermute | solution.py:45
  121.5 1.8 %collective-permute-start.3 = (f32[3,6,8,1]{3,2,1,0:T(8,128)S(1)}, f32[3,6,8,1]{3,2,1,0:T(8,128)S(1)}, u32[]{:S(2)}, u32[]{:S(2)}) collective-permute-start(f32[3,6,8,1]{3,2,1,0:T(8,128)S(1)} %slice_bitcast_fusion.2), channel_id=1, source_target_pairs={{0,1},{1,2},{2,3},{3,0},{4,5},{5,6},{6,7},{7,4},{8,9},{9,10},{10,1... | collective-permute-start | bytes 1736 | tf_op jit(solution)/shard_map/ppermute | solution.py:45
  123.3 4.3 %collective-permute-done.3 = f32[3,6,8,1]{3,2,1,0:T(8,128)S(1)} collective-permute-done((f32[3,6,8,1]{3,2,1,0:T(8,128)S(1)}, f32[3,6,8,1]{3,2,1,0:T(8,128)S(1)}, u32[]{:S(2)}, u32[]{:S(2)}) %collective-permute-start.3) | collective-permute-done | bytes 608 | tf_op jit(solution)/shard_map/ppermute | solution.py:45
  127.8 3.0 %copy.100 = f32[3,8,6,64,6]{4,3,2,1,0:T(8,128)} copy(f32[3,8,6,64,6]{3,1,4,2,0:T(8,128)S(1)} %bitcast.288) | data formatting | bytes 442368 | tf_op jit(solution)/shard_map/transpose | solution.py:123
  130.7 4.9 %broadcast_in_dim_reshape.4 = f32[1,3,48,384]{3,2,1,0:T(8,128)} reshape(f32[3,8,6,64,6]{4,3,2,1,0:T(8,128)} %copy.100) | data formatting | bytes 442368 | tf_op jit(solution)/shard_map/broadcast_in_dim;reshape | solution.py:155
  (91 shorter events, 16.1 us)
Async XLA Ops:
  0.0 12.6 %copy-start.1 = (f32[6,7]{1,0:T(8,128)S(1)}, f32[6,7]{1,0:T(8,128)}, u32[]{:S(2)}) copy-start(f32[6,7]{1,0:T(8,128)} %constant.323) | copy-start | bytes 508
  0.0 12.7 %copy-start.3 = (f32[6]{0:T(128)S(1)}, f32[6]{0:T(128)}, u32[]{:S(2)}) copy-start(f32[6]{0:T(128)} %constant.228.clone) | copy-start | bytes 76
  0.0 11.2 %copy-start = (f32[1,2,36,256]{3,1,2,0:T(2,128)S(1)}, f32[1,2,36,256]{3,1,2,0:T(2,128)}, u32[]{:S(2)}) copy-start(f32[1,2,36,256]{3,1,2,0:T(2,128)} %param.12) | copy-start | bytes 221188
  0.0 11.7 %copy-start.2 = (s32[1,256,1]{1,2,0:T(1,128)S(1)}, s32[1,256,1]{1,2,0:T(1,128)}, u32[]{:S(2)}) copy-start(s32[1,256,1]{1,2,0:T(1,128)} %param.14) | copy-start | bytes 3076
  4.9 19.1 %copy-start.4 = (s32[1,256]{1,0:T(1,128)S(1)}, s32[1,256]{1,0:T(1,128)}, u32[]{:S(2)}) copy-start(s32[1,256]{1,0:T(1,128)} %param.13) | copy-start | bytes 3076
  6.0 11.2 %all-to-all-start = ((f32[3,49,4,96]{3,1,0,2:T(8,128)}), f32[3,49,4,96]{3,1,0,2:T(8,128)S(1)}, u32[]{:S(2)}, u32[]{:S(2)}) async-start(f32[3,49,4,96]{3,1,0,2:T(8,128)} %broadcast_select_fusion), calls=%async_computation | async-start | bytes 688128 | tf_op jit(solution)/shard_map/all_to_all | solution.py:107
  19.1 11.5 %all-to-all-start.1 = ((f32[4,1,14112]{2,1,0:T(1,128)}), f32[4,1,14112]{2,1,0:T(1,128)S(1)}, u32[]{:S(2)}, u32[]{:S(2)}) async-start(f32[4,1,14112]{2,1,0:T(1,128)} %reshape.1157), calls=%async_computation.1 | async-start | bytes 454656 | tf_op jit(solution)/shard_map/all_to_all | solution.py:106
  33.5 5.8 %collective-permute-start = (f32[3,49,4,96]{3,2,1,0:T(4,128)S(1)}, f32[3,49,4,96]{3,2,1,0:T(4,128)S(1)}, u32[]{:S(2)}, u32[]{:S(2)}) collective-permute-start(f32[3,49,4,96]{3,2,1,0:T(4,128)S(1)} %copy.79), channel_id=1, source_target_pairs={{0,16},{16,0},{1,17},{17,1},{2,18},{18,2},{3,19},{19,3},{4,20},{20... | collective-permute-start | bytes 677384 | tf_op jit(solution)/shard_map/ppermute | solution.py:40
  72.3 1.7 %collective-permute-start.1 = (f32[3,49,384]{2,1,0:T(8,128)S(1)}, f32[3,49,384]{2,1,0:T(8,128)S(1)}, u32[]{:S(2)}, u32[]{:S(2)}) collective-permute-start(f32[3,49,384]{2,1,0:T(8,128)S(1)} %copy.93), channel_id=1, source_target_pairs={{0,16},{16,0},{1,17},{17,1},{2,18},{18,2},{3,19},{19,3},{4,20},{20... | collective-permute-start | bytes 677384 | tf_op jit(solution)/shard_map/ppermute | solution.py:40
  85.9 12.7 %all-to-all-start.3 = ((f32[4,1,14112]{2,1,0:T(1,128)}), f32[4,1,14112]{2,1,0:T(1,128)S(1)}, u32[]{:S(2)}, u32[]{:S(2)}) async-start(f32[4,1,14112]{2,1,0:T(1,128)} %reshape.1159), calls=%async_computation.3 | async-start | bytes 454656 | tf_op jit(solution)/shard_map/all_to_all | solution.py:106
  116.7 4.6 %collective-permute-start.2 = (f32[3,7,1,64]{3,2,1,0:T(1,128)S(1)}, f32[3,7,1,64]{3,2,1,0:T(1,128)S(1)}, u32[]{:S(2)}, u32[]{:S(2)}) collective-permute-start(f32[3,7,1,64]{3,2,1,0:T(1,128)S(1)} %slice_bitcast_fusion.3), channel_id=1, source_target_pairs={{0,4},{4,8},{8,12},{12,0},{1,5},{5,9},{9,13},{13,1},{2,6},{6,10},{... | collective-permute-start | bytes 16136 | tf_op jit(solution)/shard_map/ppermute | solution.py:45
  121.5 6.2 %collective-permute-start.3 = (f32[3,6,8,1]{3,2,1,0:T(8,128)S(1)}, f32[3,6,8,1]{3,2,1,0:T(8,128)S(1)}, u32[]{:S(2)}, u32[]{:S(2)}) collective-permute-start(f32[3,6,8,1]{3,2,1,0:T(8,128)S(1)} %slice_bitcast_fusion.2), channel_id=1, source_target_pairs={{0,1},{1,2},{2,3},{3,0},{4,5},{5,6},{6,7},{7,4},{8,9},{9,10},{10,1... | collective-permute-start | bytes 1736 | tf_op jit(solution)/shard_map/ppermute | solution.py:45
where the time goes:
time: 136 us
  other arithmetic  38.6 us (28%)
  local copies, waits for them, and re-layouts  33.6 us (25%)
  waiting for transfers between devices  18.1 us (13%)
  matrix products  18 us (13%)
  starting transfers between devices  17 us (12%)
  blocking collectives  9.92 us (7%)
    scatter-add x1, other arithmetic, local(): element_force = element_force + jnp.zeros((3, 49, segment_count), jnp.flo...  14.2 us
    all_to_all x1, blocking collectives, across_tiles(): lax.all_to_all(buffer, 'gx', split_axis=2, concat_axis=2, tiled=True)  9.92 us
    dot_general x1, matrix products, pair_forces(): jnp.einsum('lqp,cklp->ckqp', second_basis, master_grid, precision=highest)  8.66 us
    all_to_all x2, starting transfers between devices, across_tiles(): lax.all_to_all(lax.all_to_all(buffer, 'gx', split_axis=2, concat_axis=2,...  8.47 us
    scatter-add x1, other arithmetic, local(): jnp.zeros((3, 49, segment_count), jnp.float32).at[:, :, pair_slave[0]]  8.33 us
    scatter-add x1, other arithmetic, local(): jnp.zeros((3, 49, slots_total), jnp.float32).at[:, :, slot_index]  8.32 us
    ppermute x2, waiting for transfers between devices, from_behind(): lax.ppermute(value, axis, [(i, (i + by) % length) for i in range(length)])  8.06 us
    dot_general x1, matrix products, pair_forces(): jnp.einsum('kqp,clqp->cklp', first_basis, weighted, precision=highest)  7.45 us
  transfers between devices with their start and end apart: 7, of which 5 were waited for; matrix products, arithmetic and copies ran while one was open for 14% of the time, Pallas kernels for 0%

commit v1 on v0

v1 whole, which is shorter than its diff:
```python
import functools

import jax
import jax.numpy as jnp
import numpy as np
from jax import lax
from jax.experimental import pallas as pl
from jax.experimental.pallas import tpu as pltpu
from jax.sharding import PartitionSpec as P

SX = 8
SY = 64
KAPPA = 2.0
SHEAR = 1.0
LOBATTO_POINTS = (
    -1.0,
    -0.830223896278567,
    -0.4688487934707142,
    0.0,
    0.4688487934707142,
    0.830223896278567,
    1.0,
)
GAUSS_POINTS = (
    -0.932469514203152,
    -0.6612093864662645,
    -0.2386191860831969,
    0.2386191860831969,
    0.6612093864662645,
    0.932469514203152,
)
GAUSS_WEIGHTS = (
    0.1713244923791704,
    0.3607615730481386,
    0.467913934572691,
    0.467913934572691,
    0.3607615730481386,
    0.1713244923791704,
)
MESH = pl.DeviceIdType.MESH
F32 = jnp.float32
BF16 = jnp.bfloat16
NODES = 49
VALUES = 3 * NODES
LANES = 128
TAIL = VALUES - LANES
STRIDE = LANES // 6
ROWS = 160
QUADS = 36
QPAD = 40
SCALE = tuple(
    1.0 / float(np.prod([LOBATTO_POINTS[k] - LOBATTO_POINTS[m] for m in range(7) if m != k]))
    for k in range(7)
)


def tables():
    gauss = np.array(GAUSS_POINTS)
    single = np.ones((6, 7))
    for k in range(7):
        for m in range(7):
            if m != k:
                single[:, k] *= (gauss - LOBATTO_POINTS[m]) / (LOBATTO_POINTS[k] - LOBATTO_POINTS[m])
    slave = (single[:, None, :, None] * single[None, :, None, :]).reshape(QUADS, NODES)
    spread = np.zeros((3 * QPAD, ROWS), np.float32)
    for c in range(3):
        spread[c * QPAD : c * QPAD + QUADS, c * NODES : (c + 1) * NODES] = slave
    weights = np.array(GAUSS_WEIGHTS)
    quad = np.zeros((QPAD, LANES), np.float32)
    quad[:QUADS] = (weights[:, None] * weights[None, :]).reshape(QUADS, 1)
    order = np.zeros((7 * 24, 2 * LANES), np.float32)
    for column in range(2 * LANES):
        place = column if column < LANES else LANES + (column - LANES) % STRIDE
        if place < VALUES and column < LANES + 6 * STRIDE:
            c, k, m = place // NODES, place % NODES // 7, place % 7
            m = (place % NODES) % 7
            order[m * 24 + c * 8 + k, column] = 1
    join = np.zeros((6 * SX + 8, 8 * SX), np.float32)
    for la in range(SX):
        for k in range(7):
            join[6 * la + k, 8 * la + k] = 1
    return spread, spread.T.copy(), quad, order, join


def two(x):
    high = x.astype(BF16)
    return high, (x - high.astype(F32)).astype(BF16)


def dot(a, b):
    return jnp.dot(a, b, preferred_element_type=F32)


def dot_t(a, b):
    return lax.dot_general(a, b, (((1,), (1,)), ((), ())), preferred_element_type=F32)


def flag(condition):
    return jnp.where(condition, 1.0, 0.0).astype(BF16)


def basis(x):
    gaps = [x - r for r in LOBATTO_POINTS]
    before = [None] * 7
    after = [None] * 7
    for k in range(1, 7):
        before[k] = gaps[0] if k == 1 else before[k - 1] * gaps[k - 1]
    for k in range(5, -1, -1):
        after[k] = gaps[6] if k == 5 else after[k + 1] * gaps[k + 1]
    out = []
    for k in range(7):
        if k == 0:
            product = after[0]
        elif k == 6:
            product = before[6]
        else:
            product = before[k] * after[k]
        out.append(product * SCALE[k])
    return out


def tail_mask(shape, part):
    lane = lax.broadcasted_iota(jnp.int32, shape, 2)
    row = lax.broadcasted_iota(jnp.int32, shape, 1)
    start = STRIDE * (2 * part + jnp.where(row >= 4, 1, 0))
    return (lane >= start) & (lane < start + STRIDE)


def pack(gathered, send, tiles, slots):
    send[:, :slots, :] = gathered[:, :LANES].reshape(tiles, slots, LANES)
    tail = gathered[:, LANES:].reshape(tiles, slots, LANES)
    for group in range(-(-slots // 24)):
        total = None
        for part in range(min(3, slots // 8 - 3 * group)):
            row = 8 * (3 * group + part)
            block = tail[:, row : row + 8, :]
            block = jnp.where(tail_mask(block.shape, part), block, 0.0)
            total = block if total is None else total + block
        row = slots + 4 * group
        send[:, row : row + 4, :] = total[:, :4, :] + total[:, 4:, :]


def unpack(recv, tiles, slots):
    main = recv[:, :slots, :].reshape(tiles * slots, LANES)
    blocks = []
    for group in range(-(-slots // 24)):
        row = slots + 4 * group
        four = recv[:, row : row + 4, :]
        eight = jnp.concatenate([four, four], axis=1)
        for part in range(min(3, slots // 8 - 3 * group)):
            blocks.append(jnp.where(tail_mask(eight.shape, part), eight, 0.0))
    tail = jnp.concatenate(blocks, axis=1).reshape(tiles * slots, LANES)
    return jnp.concatenate([main.T, tail.T], axis=0)


def kernel(
    sizes,
    surf, coords, slaves, owners, lists, spread, spread_t, quad, order, join,
    out,
    s6, e12, lb1, lb2, value, tract, nodes, f6, pads, halo_row, halo_col,
    send1, recv1, send2, recv2, row_in, col_in, corner_in,
    ss1, rs1, ss2, rs2, hs, hr,
):
    wx, wy, capacity, slots, pairs, segs = sizes
    tiles = wx * wy
    body, gx, gy = lax.axis_index("body"), lax.axis_index("gx"), lax.axis_index("gy")
    other = 1 - body
    tile = gx * wy + gy
    next_x, next_y = lax.rem(gx + 1, wx), lax.rem(gy + 1, wy)
    back_x, back_y = lax.rem(gx + wx - 1, wx), lax.rem(gy + wy - 1, wy)

    barrier = pltpu.get_barrier_semaphore()

    def greet(j, carry):
        to = lax.rem(tile + j, tiles)
        pl.semaphore_signal(
            barrier, inc=1, device_id=(other, to // wy, lax.rem(to, wy)), device_id_type=MESH
        )
        return carry

    lax.fori_loop(0, tiles, greet, 0)
    for place in ((back_x, gy), (gx, back_y), (back_x, back_y)):
        pl.semaphore_signal(barrier, inc=1, device_id=(body,) + place, device_id_type=MESH)

    s6[...] = jnp.zeros_like(s6)
    for c in range(3):
        s6[c * NODES : (c + 1) * NODES, :] = surf[c]
    tail = s6[LANES:VALUES, :]
    for copy in range(1, 6):
        s6[LANES + copy * STRIDE : LANES + copy * STRIDE + TAIL, :] = tail
    high, low = two(s6[...])

    own = jnp.where(body == 0, lists[0], lists[1])
    pick = own.shape[1]
    column = jnp.broadcast_to(own, (LANES, pick)).T
    lane = lax.broadcasted_iota(jnp.int32, (pick, LANES), 1)
    list_hot = jnp.concatenate(
        [flag(column == lane + LANES * j) for j in range(segs // LANES)], axis=1
    )
    pack(dot_t(list_hot, high) + dot_t(list_hot, low), send1, tiles, slots)

    pl.semaphore_wait(barrier, tiles + 3)

    def copy_of(send, recv, ss, rs, to, land):
        return pltpu.make_async_remote_copy(
            src_ref=send.at[to],
            dst_ref=recv.at[land],
            send_sem=ss.at[to],
            recv_sem=rs.at[land],
            device_id=(other, to // wy, lax.rem(to, wy)),
            device_id_type=MESH,
        )

    def start_all(send, recv, ss, rs):
        def body_of(j, carry):
            to = lax.rem(tile + j, tiles)
            copy_of(send, recv, ss, rs, to, tile).start()
            return carry

        lax.fori_loop(0, tiles, body_of, 0)

    def wait_all(send, recv, ss, rs, arrive):
        def body_of(j, carry):
            copy = copy_of(send, recv, ss, rs, j, j)
            if arrive:
                copy.wait_recv()
            else:
                copy.wait_send()
            return carry

        lax.fori_loop(0, tiles, body_of, 0)

    start_all(send1, recv1, ss1, rs1)

    tile_row = lax.broadcasted_iota(jnp.int32, (tiles, pairs), 0)
    same = flag(tile_row == owners[...])
    earlier = flag(
        lax.broadcasted_iota(jnp.int32, (pairs, pairs), 0)
        < lax.broadcasted_iota(jnp.int32, (pairs, pairs), 1)
    )
    before = dot(same, earlier)
    rank = jnp.sum(before * same.astype(F32), axis=0, keepdims=True).astype(jnp.int32)
    slot = owners[...] * slots + rank
    slot_hot = flag(lax.broadcasted_iota(jnp.int32, (tiles * slots, pairs), 0) == slot)
    slave_hot = flag(lax.broadcasted_iota(jnp.int32, (segs, pairs), 0) == slaves[...])

    table_high, table_low = two(spread[...])
    gathered = dot(high[:ROWS], slave_hot) + dot(low[:ROWS], slave_hot)
    g_high, g_low = two(gathered)
    value[...] = dot(table_high, g_high) + (dot(table_high, g_low) + dot(table_low, g_high))

    e12[...] = jnp.zeros_like(e12)
    e12[0, :QUADS, :] = coords[0]
    e12[1, :QUADS, :] = coords[1]
    for chunk in range(QPAD // 8):
        at = slice(8 * chunk, 8 * chunk + 8)
        for axis, store in ((0, lb1), (1, lb2)):
            for k, factor in enumerate(basis(e12[axis, at, :])):
                store[k, at, :] = factor

    wide = SY * 6 + LANES
    source = lax.broadcasted_iota(jnp.int32, (7 * SY, wide), 0)
    target = jnp.minimum(lax.broadcasted_iota(jnp.int32, (7 * SY, wide), 1), 6 * SY)
    step_m = source // SY
    weave = flag(target == 6 * (source - step_m * SY) + step_m)

    wait_all(send1, recv1, ss1, rs1, True)
    master = unpack(recv1, tiles, slots)
    m_high, m_low = two(master)
    paired = dot(m_high, slot_hot) + dot(m_low, slot_hot)
    nodes[:LANES, :] = paired[:LANES]
    value_tail = paired[LANES : LANES + TAIL]
    for copy in range(1, 6):
        first = LANES + copy * STRIDE
        value_tail = value_tail + paired[first : first + TAIL]
    nodes[LANES:VALUES, :] = value_tail

    sign = 1.0 - 2.0 * body.astype(F32)
    for block in range(pairs // LANES):
        across = slice(block * LANES, (block + 1) * LANES)
        for chunk in range(QPAD // 8):
            at = slice(8 * chunk, 8 * chunk + 8)
            first = [lb1[k, at, across] for k in range(7)]
            second = [lb2[k, at, across] for k in range(7)]
            weight = quad[at, :]
            for c in range(3):
                total = None
                for k in range(7):
                    inner = None
                    for m in range(7):
                        row = c * NODES + 7 * k + m
                        term = second[m] * nodes[row : row + 1, across]
                        inner = term if inner is None else inner + term
                    term = first[k] * inner
                    total = term if total is None else total + term
                place = slice(c * QPAD + 8 * chunk, c * QPAD + 8 * chunk + 8)
                offset = total - value[place, across]
                if c < 2:
                    force = SHEAR * offset
                else:
                    gap = -sign * offset
                    soft = jnp.maximum(gap, 0.0) + jnp.log1p(jnp.exp(-jnp.abs(gap)))
                    force = -sign * KAPPA * soft
                tract[place, across] = force * weight

    f6[...] = jnp.zeros_like(f6)
    for block in range(pairs // LANES):
        across = slice(block * LANES, (block + 1) * LANES)
        for c in range(3):
            minus = -tract[c * QPAD : (c + 1) * QPAD, across]
            for m in range(7):
                weighted = lb2[m, :, across] * minus
                for k in range(7):
                    row = c * NODES + 7 * k + m
                    f6[row : row + 1, across] = jnp.sum(
                        lb1[k, :, across] * weighted, axis=0, keepdims=True
                    )
    tail = f6[LANES:VALUES, :]
    for copy in range(1, 6):
        f6[LANES + copy * STRIDE : LANES + copy * STRIDE + TAIL, :] = tail
    f_high, f_low = two(f6[...])
    pack(dot_t(slot_hot, f_high) + dot_t(slot_hot, f_low), send2, tiles, slots)
    start_all(send2, recv2, ss2, rs2)

    t_high, t_low = two(tract[...])
    back_high, back_low = two(spread_t[...])
    slave_force = dot(back_high, t_high) + (dot(back_high, t_low) + dot(back_low, t_high))
    a_high, a_low = two(slave_force)
    s6[:ROWS, :] = dot_t(a_high, slave_hot) + dot_t(a_low, slave_hot)
    s6[ROWS:, :] = jnp.zeros((2 * LANES - ROWS, segs), F32)

    wait_all(send2, recv2, ss2, rs2, True)
    r_high, r_low = two(unpack(recv2, tiles, slots))
    element = s6[...] + (dot(r_high, list_hot) + dot(r_low, list_hot))
    e_high, e_low = two(element)
    arrange = order[...].astype(BF16)
    ordered = dot(arrange, e_high) + dot(arrange, e_low)
    for m in range(7):
        for c in range(3):
            for la in range(SX):
                pads[c, 8 * la : 8 * la + 8, m * SY : (m + 1) * SY] = ordered[
                    m * 24 + c * 8 : m * 24 + c * 8 + 8, la * SY : (la + 1) * SY
                ]
    together = join[...].astype(BF16)
    lanes = lax.broadcasted_iota(jnp.int32, (6 * SX + 8, LANES), 1)
    column = jnp.zeros((6 * SX + 8, LANES), F32)
    halo_row[...] = jnp.zeros_like(halo_row)
    for c in range(3):
        p_high, p_low = two(pads[c])
        x_high, x_low = two(dot(together, p_high) + dot(together, p_low))
        grid = dot(x_high, weave) + dot(x_low, weave)
        out[c] = grid[: 6 * SX, : 6 * SY]
        halo_row[c : c + 1, :] = grid[6 * SX : 6 * SX + 1, : 6 * SY]
        column = jnp.where(lanes == c, grid[:, 6 * SY :], column)
    halo_col[...] = column

    messages = [
        (halo_row, row_in, (next_x, gy)),
        (halo_col.at[pl.ds(0, 6 * SX)], col_in, (gx, next_y)),
        (halo_col.at[pl.ds(6 * SX, 8)], corner_in, (next_x, next_y)),
    ]
    copies = [
        pltpu.make_async_remote_copy(
            src_ref=src,
            dst_ref=dst,
            send_sem=hs.at[i],
            recv_sem=hr.at[i],
            device_id=(body,) + place,
            device_id_type=MESH,
        )
        for i, (src, dst, place) in enumerate(messages)
    ]
    for copy in copies:
        copy.start()
    wait_all(send1, recv1, ss1, rs1, False)
    wait_all(send2, recv2, ss2, rs2, False)
    for copy in copies:
        copy.wait_recv()
    first_row = lax.broadcasted_iota(jnp.int32, (8, LANES), 0) == 0
    for c in range(3):
        out[c, 0:1, :] = out[c, 0:1, :] + row_in[c : c + 1, :]
        wide_lanes = lax.broadcasted_iota(jnp.int32, (6 * SX, LANES), 1)
        edge = jnp.sum(jnp.where(wide_lanes == c, col_in[...], 0.0), axis=1, keepdims=True)
        out[c, :, :LANES] = out[c, :, :LANES] + jnp.where(wide_lanes == 0, edge, 0.0)
        corner = jnp.sum(
            jnp.where(lanes[:8] == c, corner_in[...], 0.0), axis=1, keepdims=True
        )
        out[c, :8, :LANES] = out[c, :8, :LANES] + jnp.where(
            first_row & (lanes[:8] == 0), corner, 0.0
        )
    for copy in copies:
        copy.wait_send()


def local(surface_disp, proj_coords, pair_slave, pair_owner, send_list):
    wx, wy = lax.axis_size("gx"), lax.axis_size("gy")
    tiles = wx * wy
    segs = surface_disp.shape[-1]
    pairs = proj_coords.shape[-1]
    capacity = send_list.shape[-1] // tiles
    slots = -(-capacity // 8) * 8
    lists = send_list
    if slots != capacity:
        lists = lists.reshape(2, 1, tiles, capacity)
        lists = jnp.pad(lists, ((0, 0), (0, 0), (0, 0), (0, slots - capacity)), constant_values=-1)
        lists = lists.reshape(2, 1, tiles * slots)
    block = slots + 4 * -(-slots // 24)
    spread, spread_t, quad, order, join = tables()
    sizes = (wx, wy, capacity, slots, pairs, segs)
    vmem = pl.BlockSpec(memory_space=pltpu.VMEM)
    buffer = pltpu.VMEM((tiles, block, LANES), F32)
    result = pl.pallas_call(
        functools.partial(kernel, sizes),
        out_shape=jax.ShapeDtypeStruct((3, 6 * SX, 6 * SY), F32),
        in_specs=[vmem] * 10,
        out_specs=vmem,
        scratch_shapes=[
            pltpu.VMEM((2 * LANES, segs), F32),
            pltpu.VMEM((2, QPAD, pairs), F32),
            pltpu.VMEM((7, QPAD, pairs), F32),
            pltpu.VMEM((7, QPAD, pairs), F32),
            pltpu.VMEM((3 * QPAD, pairs), F32),
            pltpu.VMEM((3 * QPAD, pairs), F32),
            pltpu.VMEM((ROWS, pairs), F32),
            pltpu.VMEM((2 * LANES, pairs), F32),
            pltpu.VMEM((3, 8 * SX, 7 * SY), F32),
            pltpu.VMEM((8, 6 * SY), F32),
            pltpu.VMEM((6 * SX + 8, LANES), F32),
            buffer,
            buffer,
            buffer,
            buffer,
            pltpu.VMEM((8, 6 * SY), F32),
            pltpu.VMEM((6 * SX, LANES), F32),
            pltpu.VMEM((8, LANES), F32),
            pltpu.SemaphoreType.DMA((tiles,)),
            pltpu.SemaphoreType.DMA((tiles,)),
            pltpu.SemaphoreType.DMA((tiles,)),
            pltpu.SemaphoreType.DMA((tiles,)),
            pltpu.SemaphoreType.DMA((3,)),
            pltpu.SemaphoreType.DMA((3,)),
        ],
        compiler_params=pltpu.CompilerParams(
            collective_id=0, has_side_effects=True, vmem_limit_bytes=48 * 1024 * 1024
        ),
    )(
        surface_disp[0],
        proj_coords[0],
        pair_slave,
        pair_owner.reshape(1, pairs),
        lists,
        spread,
        spread_t,
        quad,
        order,
        join,
    )
    return result[None]


def solution(mesh):
    return jax.shard_map(
        local,
        mesh=mesh,
        in_specs=(
            P("body", None, None, ("gx", "gy")),
            P("body", None, None, ("gx", "gy")),
            P("body", ("gx", "gy")),
            P("body", ("gx", "gy"), None),
            P(None, ("gx", "gy"), None),
        ),
        out_specs=P("body", None, "gx", "gy"),
        check_vma=False,
    )
```

time: 136 us -> 33.8 us (0.25)
  other arithmetic: 38.6 us -> 0 us
  local copies, waits for them, and re-layouts: 33.6 us -> 3.32 us
  Pallas kernels: 0 us -> 30.2 us
  waiting for transfers between devices: 18.1 us -> 0 us
  matrix products: 18 us -> 0 us
  starting transfers between devices: 17 us -> 0 us
  blocking collectives: 9.92 us -> 0 us
    scatter-add x5 -> x0, other arithmetic: 31 us -> none  [the longest x1 14.2 us: local(): element_force = element_force + jnp.zeros((3, 49, segment_count), jnp.flo...]
    pallas_call x0 -> x1, Pallas kernels: none -> 30.2 us  [local(): pl.pallas_call(functools.partial(kernel, sizes), out_shape=jax.ShapeDtype...]
    dot_general x4 -> x0, matrix products: 18 us -> none  [the longest x1 8.66 us: pair_forces(): jnp.einsum('lqp,cklp->ckqp', second_basis, master_grid, precision=highest)]
    all_to_all x3 -> x0, starting transfers between devices: 13.7 us -> none  [the longest x2 8.47 us: across_tiles(): lax.all_to_all(lax.all_to_all(buffer, 'gx', split_axis=2, concat_axis=2,...]
    another operation x9 -> x0, local copies, waits for them, and re-layouts: 10.8 us -> none  [the longest x4 5.46 us: basis_traced(): return jnp.stack(factors)]
    all_to_all x1 -> x0, blocking collectives: 9.92 us -> none  [across_tiles(): lax.all_to_all(buffer, 'gx', split_axis=2, concat_axis=2, tiled=True)]
    ppermute x4 -> x0, waiting for transfers between devices: 9.22 us -> none  [the longest x2 8.06 us: from_behind(): lax.ppermute(value, axis, [(i, (i + by) % length) for i in range(length)])]
    all_to_all x3 -> x0, waiting for transfers between devices: 8.86 us -> none  [the longest x2 4.48 us: across_tiles(): lax.all_to_all(lax.all_to_all(buffer, 'gx', split_axis=2, concat_axis=2,...]
  transfers between devices with their start and end apart: 7 -> 0, of which waited for: 5 -> 0; matrix products, arithmetic and copies ran while one was open for 14% -> 0% of each run, Pallas kernels for 0% -> 0%
where the time goes in v1:
time: 33.8 us; the launch traced here: 33.6 us
  Pallas kernels  30.2 us (89%)
  local copies, waits for them, and re-layouts  3.32 us (10%)
    pallas_call x1, Pallas kernels, local(): pl.pallas_call(functools.partial(kernel, sizes), out_shape=jax.ShapeDtype...  30.2 us
    unnamed x19, local copies, waits for them, and re-layouts  3.32 us

profile of v1, /device:TPU:0, one launch (start us, length us, event | category | flops | bytes accessed | tf_op | source)
XLA Modules:
  0.0 33.6 jit_solution(9108764604736901683)
XLA Ops:
  0.0 0.9 %copy.16 = f32[1,2,36,256]{3,2,1,0:T(8,128)S(1)} copy(f32[1,2,36,256]{3,1,2,0:T(2,128)} %param.11) | data formatting | bytes 147456 | tf_op args[1]
  0.9 0.0 copy-start
  0.9 0.0 copy-start.1
  0.9 0.0 copy-start.2
  0.9 0.0 copy-start.3
  0.9 0.0 copy-start.4
  0.9 0.0 copy-start.5
  1.0 0.0 copy-start.7
  1.0 1.1 %copy.15 = f32[1,3,49,512]{3,2,0,1:T(8,128)S(1)} copy(f32[1,3,49,512]{3,0,2,1:T(1,128)} %param.10) | data formatting | bytes 602112
  2.1 0.0 copy-start.6
  2.1 0.0 copy-done
  2.1 0.0 copy-done.1
  2.1 0.0 copy-done.2
  2.1 0.0 copy-done.3
  2.1 0.0 copy-done.4
  2.1 0.0 copy-done.5
  2.1 0.0 copy-done.7
  2.1 0.6 %copy-done.6 = s32[1,256]{1,0:T(1,128)S(1)} copy-done((s32[1,256]{1,0:T(1,128)S(1)}, s32[1,256]{1,0:T(1,128)}, u32[]{:S(2)}) %copy-start.6) | copy-done | bytes 1048
  2.7 30.2 %shard_map.100 = f32[3,48,384]{2,1,0:T(8,128)S(1)} custom-call(f32[3,49,512]{2,1,0:T(8,128)S(1)} %bitcast.8, f32[2,36,256]{2,1,0:T(8,128)S(1)} %bitcast.10, s32[1,256]{1,0:T(1,128)S(1)} %copy-done.6, s32[1,256]{1,0:T(1,128)S(1)} %bitcast.11, s32[2,1,384]{2,1,0:T(1,128)S(1)} %copy-done.5, f32[120,160]{1,0:T(8,128)S(1)} %copy-done.1, ...), custom_call_target="tpu_custom_call" | custom-call | tf_op jit(solution)/shard_map/pallas_call | solution.py:412
  32.9 0.7 %copy.18 = f32[1,3,48,384]{3,2,1,0:T(8,128)} copy(f32[1,3,48,384]{3,2,1,0:T(8,128)S(1)} %bitcast.9) | data formatting | bytes 442368
Async XLA Ops:
  0.9 1.2 %copy-start = (f32[168,256]{1,0:T(8,128)S(1)}, f32[168,256]{1,0:T(8,128)}, u32[]{:S(2)}) copy-start(f32[168,256]{1,0:T(8,128)} %constant.13.clone.order) | copy-start | bytes 516100
  0.9 1.2 %copy-start.1 = (f32[120,160]{1,0:T(8,128)S(1)}, f32[120,160]{1,0:T(8,128)}, u32[]{:S(2)}) copy-start(f32[120,160]{1,0:T(8,128)} %constant.10.clone.spread) | copy-start | bytes 230404
  0.9 1.2 %copy-start.2 = (f32[160,120]{1,0:T(8,128)S(1)}, f32[160,120]{1,0:T(8,128)}, u32[]{:S(2)}) copy-start(f32[160,120]{1,0:T(8,128)} %constant.11.clone.spread_t) | copy-start | bytes 230404
  0.9 1.2 %copy-start.3 = (f32[56,64]{1,0:T(8,128)S(1)}, f32[56,64]{1,0:T(8,128)}, u32[]{:S(2)}) copy-start(f32[56,64]{1,0:T(8,128)} %constant.14.clone.join) | copy-start | bytes 43012
  0.9 1.2 %copy-start.4 = (f32[40,128]{1,0:T(8,128)S(1)}, f32[40,128]{1,0:T(8,128)}, u32[]{:S(2)}) copy-start(f32[40,128]{1,0:T(8,128)} %constant.12.clone.quad) | copy-start | bytes 61444
  0.9 1.2 %copy-start.5 = (s32[2,1,384]{2,1,0:T(1,128)S(1)}, s32[2,1,384]{2,1,0:T(1,128)}, u32[]{:S(2)}) copy-start(s32[2,1,384]{2,1,0:T(1,128)} %lists.1) | copy-start | bytes 9220
  1.0 1.2 %copy-start.7 = (s32[1,256,1]{1,2,0:T(1,128)S(1)}, s32[1,256,1]{1,2,0:T(1,128)}, u32[]{:S(2)}) copy-start(s32[1,256,1]{1,2,0:T(1,128)} %param.13) | copy-start | bytes 3076
  2.1 0.7 %copy-start.6 = (s32[1,256]{1,0:T(1,128)S(1)}, s32[1,256]{1,0:T(1,128)}, u32[]{:S(2)}) copy-start(s32[1,256]{1,0:T(1,128)} %slaves.1) | copy-start | bytes 3076

commit v2 on v1

v2 whole, which is shorter than its diff:
```python
import functools

import jax
import jax.numpy as jnp
import numpy as np
from jax import lax
from jax.experimental import pallas as pl
from jax.experimental.pallas import tpu as pltpu
from jax.sharding import PartitionSpec as P

SX = 8
SY = 64
KAPPA = 2.0
SHEAR = 1.0
LOBATTO_POINTS = (
    -1.0,
    -0.830223896278567,
    -0.4688487934707142,
    0.0,
    0.4688487934707142,
    0.830223896278567,
    1.0,
)
GAUSS_POINTS = (
    -0.932469514203152,
    -0.6612093864662645,
    -0.2386191860831969,
    0.2386191860831969,
    0.6612093864662645,
    0.932469514203152,
)
GAUSS_WEIGHTS = (
    0.1713244923791704,
    0.3607615730481386,
    0.467913934572691,
    0.467913934572691,
    0.3607615730481386,
    0.1713244923791704,
)
MESH = pl.DeviceIdType.MESH
F32 = jnp.float32
BF16 = jnp.bfloat16
NODES = 49
NPAD = 56
LANES = 128
HEAD = 40
TAIL = NODES - HEAD
QUADS = 36
QPAD = 40
BLOCK = 10
SCALE = tuple(
    1.0 / float(np.prod([LOBATTO_POINTS[k] - LOBATTO_POINTS[m] for m in range(7) if m != k]))
    for k in range(7)
)


def tables():
    gauss = np.array(GAUSS_POINTS)
    single = np.ones((6, 7))
    for k in range(7):
        for m in range(7):
            if m != k:
                single[:, k] *= (gauss - LOBATTO_POINTS[m]) / (LOBATTO_POINTS[k] - LOBATTO_POINTS[m])
    spread = np.zeros((QPAD, NPAD), np.float32)
    spread[:QUADS, :NODES] = (single[:, None, :, None] * single[None, :, None, :]).reshape(
        QUADS, NODES
    )
    weights = np.array(GAUSS_WEIGHTS)
    quad = np.zeros((QPAD, LANES), np.float32)
    quad[:QUADS] = (weights[:, None] * weights[None, :]).reshape(QUADS, 1)
    tile = np.zeros((LANES, 16), np.float32)
    for copy in range(12):
        for j in range(TAIL):
            tile[copy * TAIL + j, j] = 1
    join = np.zeros((6 * SX + 8, 8 * SX), np.float32)
    for la in range(SX):
        for k in range(7):
            join[6 * la + k, 8 * la + k] = 1
    return spread, spread.T.copy(), quad, tile, tile.T.copy(), join


def two(x):
    high = x.astype(BF16)
    return high, (x - high.astype(F32)).astype(BF16)


def dot(a, b):
    return jnp.dot(a, b, preferred_element_type=F32)


def dot_t(a, b):
    return lax.dot_general(a, b, (((1,), (1,)), ((), ())), preferred_element_type=F32)


def flag(condition):
    return jnp.where(condition, 1.0, 0.0).astype(BF16)


def basis(x):
    gaps = [x - r for r in LOBATTO_POINTS]
    before = [None] * 7
    after = [None] * 7
    for k in range(1, 7):
        before[k] = gaps[0] if k == 1 else before[k - 1] * gaps[k - 1]
    for k in range(5, -1, -1):
        after[k] = gaps[6] if k == 5 else after[k + 1] * gaps[k + 1]
    out = []
    for k in range(7):
        if k == 0:
            product = after[0]
        elif k == 6:
            product = before[6]
        else:
            product = before[k] * after[k]
        out.append(product * SCALE[k])
    return out


def head_mask(shape, part):
    lane = lax.broadcasted_iota(jnp.int32, shape, 1)
    return (lane >= HEAD * part) & (lane < HEAD * (part + 1))


def tail_mask(shape, part):
    lane = lax.broadcasted_iota(jnp.int32, shape, 2)
    row = lax.broadcasted_iota(jnp.int32, shape, 1)
    start = TAIL * (4 * part + row // 2)
    return (lane >= start) & (lane < start + TAIL)


def pack(rows, hot, tile, send, tiles, parts):
    first = rows[:HEAD]
    head = jnp.concatenate(
        [first, first, first, jnp.zeros((LANES - 3 * HEAD, first.shape[1]), F32)], axis=0
    )
    gathered = None
    for piece, tail in zip(two(head), two(rows[HEAD:])):
        both = jnp.concatenate([piece, dot(tile, tail).astype(BF16)], axis=0)
        term = dot_t(hot, both)
        gathered = term if gathered is None else gathered + term
    count = 8 * tiles
    for group in range(-(-parts // 3)):
        heads, tails = None, None
        for part in range(min(3, parts - 3 * group)):
            at = (3 * group + part) * count
            block = gathered[at : at + count, :LANES]
            block = jnp.where(head_mask(block.shape, part), block, 0.0)
            heads = block if heads is None else heads + block
            block = gathered[at : at + count, LANES:].reshape(tiles, 8, LANES)
            block = jnp.where(tail_mask(block.shape, part), block, 0.0)
            tails = block if tails is None else tails + block
        at = BLOCK * group
        send[:, at : at + 8, :] = heads.reshape(tiles, 8, LANES)
        send[:, at + 8 : at + 10, :] = (tails[:, 0:2] + tails[:, 2:4]) + (
            tails[:, 4:6] + tails[:, 6:8]
        )


def unpack(recv, fold, tiles, parts):
    count = 8 * tiles
    firsts, lasts = [], []
    for group in range(-(-parts // 3)):
        at = BLOCK * group
        turned = recv[:, at : at + 8, :].reshape(count, LANES).T
        pair = recv[:, at + 8 : at + 10, :]
        eight = jnp.concatenate([pair] * 4, axis=1)
        for part in range(min(3, parts - 3 * group)):
            firsts.append(turned[part * HEAD : (part + 1) * HEAD])
            lasts.append(
                jnp.where(tail_mask(eight.shape, part), eight, 0.0).reshape(count, LANES)
            )
    last = jnp.concatenate(lasts, axis=0)
    high, low = two(last)
    return jnp.concatenate(
        [jnp.concatenate(firsts, axis=1), dot_t(fold, high) + dot_t(fold, low)], axis=0
    )


def kernel(
    sizes,
    surf, coords, slaves, owners, lists, spread, spread_t, quad, tile_in, fold_in, join,
    out,
    held, lb1, lb2, value, tract, nodes, force_rows, elements, strips, pads,
    send1, recv1, send2, recv2, row_out, col_out, row_in, col_in, corner_in,
    ss1, rs1, ss2, rs2, hs, hr,
):
    wx, wy, parts, pairs, segs = sizes
    tiles = wx * wy
    body, gx, gy = lax.axis_index("body"), lax.axis_index("gx"), lax.axis_index("gy")
    other = 1 - body
    here = gx * wy + gy
    next_x, next_y = lax.rem(gx + 1, wx), lax.rem(gy + 1, wy)
    back_x, back_y = lax.rem(gx + wx - 1, wx), lax.rem(gy + wy - 1, wy)

    barrier = pltpu.get_barrier_semaphore()

    def greet(j, carry):
        to = lax.rem(here + j, tiles)
        pl.semaphore_signal(
            barrier, inc=1, device_id=(other, to // wy, lax.rem(to, wy)), device_id_type=MESH
        )
        return carry

    lax.fori_loop(0, tiles, greet, 0)
    for place in ((back_x, gy), (gx, back_y), (back_x, back_y)):
        pl.semaphore_signal(barrier, inc=1, device_id=(body,) + place, device_id_type=MESH)

    tile = tile_in[...].astype(BF16)
    fold = fold_in[...].astype(BF16)

    own = jnp.where(body == 0, lists[0], lists[1])
    pick = own.shape[1]
    column = jnp.broadcast_to(own, (LANES, pick)).T.reshape(tiles, parts, 8, LANES)
    column = jnp.concatenate(
        [column[:, part].reshape(8 * tiles, LANES) for part in range(parts)], axis=0
    )
    lane = lax.broadcasted_iota(jnp.int32, (pick, LANES), 1)
    list_hot = jnp.concatenate(
        [flag(column == lane + LANES * j) for j in range(segs // LANES)], axis=1
    )

    def copy_of(c, send, recv, ss, rs, to, land):
        return pltpu.make_async_remote_copy(
            src_ref=send.at[c, to],
            dst_ref=recv.at[c, land],
            send_sem=ss.at[c, to],
            recv_sem=rs.at[c, land],
            device_id=(other, to // wy, lax.rem(to, wy)),
            device_id_type=MESH,
        )

    def start_all(*where):
        def step(j, carry):
            copy_of(*where, lax.rem(here + j, tiles), here).start()
            return carry

        lax.fori_loop(0, tiles, step, 0)

    def wait_all(*where, arrive):
        def step(j, carry):
            copy = copy_of(*where, j, j)
            if arrive:
                copy.wait_recv()
            else:
                copy.wait_send()
            return carry

        lax.fori_loop(0, tiles, step, 0)

    there = (send1, recv1, ss1, rs1)
    back = (send2, recv2, ss2, rs2)

    held[...] = jnp.zeros_like(held)
    for c in range(3):
        held[c, :NODES, :] = surf[c * NODES : (c + 1) * NODES, 0, :]
        pack(held[c], list_hot, tile, send1.at[c], tiles, parts)
        if c == 0:
            pl.semaphore_wait(barrier, tiles + 3)
        start_all(c, *there)

    tile_row = lax.broadcasted_iota(jnp.int32, (tiles, pairs), 0)
    same = flag(tile_row == owners[...])
    earlier = flag(
        lax.broadcasted_iota(jnp.int32, (pairs, pairs), 0)
        < lax.broadcasted_iota(jnp.int32, (pairs, pairs), 1)
    )
    before = dot(same, earlier)
    rank = jnp.sum(before * same.astype(F32), axis=0, keepdims=True).astype(jnp.int32)
    part_of = rank // 8
    slot = part_of * (8 * tiles) + owners[...] * 8 + (rank - 8 * part_of)
    slot_hot = flag(lax.broadcasted_iota(jnp.int32, (8 * tiles * parts, pairs), 0) == slot)
    slave_hot = flag(lax.broadcasted_iota(jnp.int32, (segs, pairs), 0) == slaves[...])

    table_high, table_low = two(spread[...])
    back_high, back_low = two(spread_t[...])
    for c in range(3):
        high, low = two(held[c])
        high, low = two(dot(high, slave_hot) + dot(low, slave_hot))
        value[c] = dot(table_high, high) + (dot(table_high, low) + dot(table_low, high))

    for axis, store in ((0, lb1), (1, lb2)):
        place = jnp.concatenate(
            [coords[:, axis, :], jnp.zeros((QPAD - QUADS, pairs), F32)], axis=0
        )
        for chunk in range(QPAD // 8):
            at = slice(8 * chunk, 8 * chunk + 8)
            for k, factor in enumerate(basis(place[at])):
                store[k, at, :] = factor

    wide = SY * 6
    source = lax.broadcasted_iota(jnp.int32, (7 * SY, wide), 0)
    target = lax.broadcasted_iota(jnp.int32, (7 * SY, wide), 1)
    step_m = source // SY
    weave = flag(target == 6 * (source - step_m * SY) + step_m)
    together = join[...].astype(BF16)

    pads[...] = jnp.zeros_like(pads)
    force_rows[...] = jnp.zeros_like(force_rows)
    sign = 1.0 - 2.0 * body.astype(F32)
    blocks = [slice(b * LANES, (b + 1) * LANES) for b in range(pairs // LANES)]

    for c in range(3):
        wait_all(c, *there, arrive=True)
        high, low = two(unpack(recv1.at[c], fold, tiles, parts))
        nodes[...] = dot(high, slot_hot) + dot(low, slot_hot)
        for across in blocks:
            for chunk in range(QPAD // 8):
                at = slice(8 * chunk, 8 * chunk + 8)
                second = [lb2[k, at, across] for k in range(7)]
                total = None
                for k in range(7):
                    inner = None
                    for m in range(7):
                        row = 7 * k + m
                        term = second[m] * nodes[row : row + 1, across]
                        inner = term if inner is None else inner + term
                    term = lb1[k, at, across] * inner
                    total = term if total is None else total + term
                offset = total - value[c, at, across]
                if c < 2:
                    force = SHEAR * offset
                else:
                    gap = -sign * offset
                    soft = jnp.maximum(gap, 0.0) + jnp.log1p(jnp.exp(-jnp.abs(gap)))
                    force = -sign * KAPPA * soft
                tract[c, at, across] = force * quad[at, :]
        for across in blocks:
            minus = -tract[c, :, across]
            for m in range(7):
                weighted = lb2[m, :, across] * minus
                for k in range(7):
                    row = 7 * k + m
                    force_rows[row : row + 1, across] = jnp.sum(
                        lb1[k, :, across] * weighted, axis=0, keepdims=True
                    )
        pack(force_rows[...], slot_hot, tile, send2.at[c], tiles, parts)
        start_all(c, *back)

    for c in range(3):
        high, low = two(tract[c])
        slave_force = dot(back_high, high) + (dot(back_high, low) + dot(back_low, high))
        high, low = two(slave_force)
        elements[c] = dot_t(high, slave_hot) + dot_t(low, slave_hot)

    halos = []
    for c in range(3):
        wait_all(c, *back, arrive=True)
        high, low = two(unpack(recv2.at[c], fold, tiles, parts))
        total = elements[c] + (dot(high, list_hot) + dot(low, list_hot))
        for block in range(segs // LANES):
            strips[block] = total[:, block * LANES : (block + 1) * LANES]
        for m in range(7):
            for la in range(SX):
                block, lane = la * SY // LANES, la * SY % LANES
                rows = strips[block, pl.ds(m, 8, stride=7), :]
                pads[8 * la : 8 * la + 8, m * SY : (m + 1) * SY] = rows[:, lane : lane + SY]
        high, low = two(pads[...])
        joined = dot(together, high) + dot(together, low)
        col_out[c] = joined[:, 7 * SY - LANES :].T[LANES - 1 :, :]
        high, low = two(joined)
        grid = dot(high, weave) + dot(low, weave)
        out[c] = grid[: 6 * SX]
        row_out[c] = grid[6 * SX : 6 * SX + 1]
        messages = [
            (row_out.at[c], row_in.at[c], (next_x, gy)),
            (col_out.at[c], col_in.at[c], (gx, next_y)),
            (col_out.at[c], corner_in.at[c], (next_x, next_y)),
        ]
        for i, (src, dst, place) in enumerate(messages):
            copy = pltpu.make_async_remote_copy(
                src_ref=src,
                dst_ref=dst,
                send_sem=hs.at[c, i],
                recv_sem=hr.at[c, i],
                device_id=(body,) + place,
                device_id_type=MESH,
            )
            copy.start()
            halos.append(copy)

    for c in range(3):
        wait_all(c, *there, arrive=False)
        wait_all(c, *back, arrive=False)
    lanes = lax.broadcasted_iota(jnp.int32, (1, LANES), 1)
    for c in range(3):
        for copy in halos[3 * c : 3 * c + 3]:
            copy.wait_recv()
        corner = jnp.sum(
            jnp.where(lanes[:, : 6 * SX + 8] == 6 * SX, corner_in[c], 0.0), axis=1, keepdims=True
        )
        row = row_in[c]
        out[c, 0:1, :] = out[c, 0:1, :] + row
        edge = jnp.broadcast_to(col_in[c], (LANES, 6 * SX + 8)).T[: 6 * SX]
        first = (lax.broadcasted_iota(jnp.int32, edge.shape, 0) == 0).astype(F32)
        left = lax.broadcasted_iota(jnp.int32, edge.shape, 1) == 0
        out[c, :, :LANES] = out[c, :, :LANES] + jnp.where(left, edge + first * corner, 0.0)
    for copy in halos:
        copy.wait_send()


def local(surface_disp, proj_coords, pair_slave, pair_owner, send_list):
    wx, wy = lax.axis_size("gx"), lax.axis_size("gy")
    tiles = wx * wy
    segs = surface_disp.shape[-1]
    pairs = proj_coords.shape[-1]
    capacity = send_list.shape[-1] // tiles
    parts = -(-capacity // 8)
    slots = 8 * parts
    lists = send_list
    if slots != capacity:
        lists = lists.reshape(2, 1, tiles, capacity)
        lists = jnp.pad(lists, ((0, 0), (0, 0), (0, 0), (0, slots - capacity)), constant_values=-1)
        lists = lists.reshape(2, 1, tiles * slots)
    sizes = (wx, wy, parts, pairs, segs)
    vmem = pl.BlockSpec(memory_space=pltpu.VMEM)
    buffer = pltpu.VMEM((3, tiles, BLOCK * -(-parts // 3), LANES), F32)
    result = pl.pallas_call(
        functools.partial(kernel, sizes),
        out_shape=jax.ShapeDtypeStruct((3, 6 * SX, 6 * SY), F32),
        in_specs=[vmem] * 11,
        out_specs=vmem,
        scratch_shapes=[
            pltpu.VMEM((3, NPAD, segs), F32),
            pltpu.VMEM((7, QPAD, pairs), F32),
            pltpu.VMEM((7, QPAD, pairs), F32),
            pltpu.VMEM((3, QPAD, pairs), F32),
            pltpu.VMEM((3, QPAD, pairs), F32),
            pltpu.VMEM((NPAD, pairs), F32),
            pltpu.VMEM((NPAD, pairs), F32),
            pltpu.VMEM((3, NPAD, segs), F32),
            pltpu.VMEM((segs // LANES, NPAD, LANES), F32),
            pltpu.VMEM((8 * SX, 7 * SY), F32),
            buffer,
            buffer,
            buffer,
            buffer,
            pltpu.VMEM((3, 1, 6 * SY), F32),
            pltpu.VMEM((3, 1, 6 * SX + 8), F32),
            pltpu.VMEM((3, 1, 6 * SY), F32),
            pltpu.VMEM((3, 1, 6 * SX + 8), F32),
            pltpu.VMEM((3, 1, 6 * SX + 8), F32),
            pltpu.SemaphoreType.DMA((3, tiles)),
            pltpu.SemaphoreType.DMA((3, tiles)),
            pltpu.SemaphoreType.DMA((3, tiles)),
            pltpu.SemaphoreType.DMA((3, tiles)),
            pltpu.SemaphoreType.DMA((3, 3)),
            pltpu.SemaphoreType.DMA((3, 3)),
        ],
        compiler_params=pltpu.CompilerParams(
            collective_id=0, has_side_effects=True, vmem_limit_bytes=48 * 1024 * 1024
        ),
    )(
        surface_disp.reshape(3 * NODES, 1, segs),
        proj_coords[0].transpose(1, 0, 2),
        pair_slave,
        pair_owner.reshape(1, pairs),
        lists,
        *tables(),
    )
    return result[None]


def solution(mesh):
    return jax.shard_map(
        local,
        mesh=mesh,
        in_specs=(
            P("body", None, None, ("gx", "gy")),
            P("body", None, None, ("gx", "gy")),
            P("body", ("gx", "gy")),
            P("body", ("gx", "gy"), None),
            P(None, ("gx", "gy"), None),
        ),
        out_specs=P("body", None, "gx", "gy"),
        check_vma=False,
    )
```

time: 33.8 us -> 35 us (1.036)
  local copies, waits for them, and re-layouts: 3.32 us -> 7.05 us
  Pallas kernels: 30.2 us -> 27.5 us
    unnamed x19 -> x23, local copies, waits for them, and re-layouts: 3.32 us -> 7.05 us
    pallas_call x1, Pallas kernels: 30.2 us -> 27.5 us  [local(): pl.pallas_call(functools.partial(kernel, sizes), out_shape=jax.ShapeDtype...]
where the time goes in v2:
time: 35 us; the launch traced here: 34.5 us
  Pallas kernels  27.5 us (79%)
  local copies, waits for them, and re-layouts  7.05 us (20%)
    pallas_call x1, Pallas kernels, local(): pl.pallas_call(functools.partial(kernel, sizes), out_shape=jax.ShapeDtype...  27.5 us
    unnamed x23, local copies, waits for them, and re-layouts  7.05 us

profile of v2, /device:TPU:0, one launch (start us, length us, event | category | flops | bytes accessed | tf_op | source)
XLA Modules:
  0.0 34.5 jit_solution(13443914592749515464)
XLA Ops:
  0.0 0.0 copy-start.7
  0.0 0.0 copy-start.8
  0.0 0.0 copy-start.10
  0.0 0.0 copy-start.9
  0.0 0.7 %copy-done.7 = f32[16,128]{1,0:T(8,128)S(1)} copy-done((f32[16,128]{1,0:T(8,128)S(1)}, f32[16,128]{1,0:T(8,128)}, u32[]{:S(2)}) %copy-start.7) | copy-done | bytes 8216
  0.7 0.0 copy-done.8
  0.7 0.0 copy-done.10
  0.7 0.0 copy-done.9
  0.7 0.0 copy-start
  0.7 1.0 %copy-done = f32[1,3,49,512]{3,0,2,1:T(1,128)S(1)} copy-done((f32[1,3,49,512]{3,0,2,1:T(1,128)S(1)}, f32[1,3,49,512]{3,0,2,1:T(1,128)}, u32[]{:S(2)}) %copy-start) | copy-done | bytes 301080
  1.7 0.0 copy-start.1
  1.7 0.9 %copy-done.1 = f32[1,2,36,256]{3,1,2,0:T(2,128)S(1)} copy-done((f32[1,2,36,256]{3,1,2,0:T(2,128)S(1)}, f32[1,2,36,256]{3,1,2,0:T(2,128)}, u32[]{:S(2)}) %copy-start.1) | copy-done | bytes 73752
  2.6 0.0 copy-start.2
  2.6 0.8 %copy-done.2 = f32[128,16]{1,0:T(8,128)S(1)} copy-done((f32[128,16]{1,0:T(8,128)S(1)}, f32[128,16]{1,0:T(8,128)}, u32[]{:S(2)}) %copy-start.2) | copy-done | bytes 8216
  3.4 0.0 copy-start.3
  3.4 0.7 %copy-done.3 = f32[56,64]{1,0:T(8,128)S(1)} copy-done((f32[56,64]{1,0:T(8,128)S(1)}, f32[56,64]{1,0:T(8,128)}, u32[]{:S(2)}) %copy-start.3) | copy-done | bytes 14360
  4.2 0.0 copy-start.4
  4.2 0.7 %copy-done.4 = f32[56,40]{1,0:T(8,128)S(1)} copy-done((f32[56,40]{1,0:T(8,128)S(1)}, f32[56,40]{1,0:T(8,128)}, u32[]{:S(2)}) %copy-start.4) | copy-done | bytes 8984
  4.9 0.0 copy-start.5
  4.9 0.7 %copy-done.5 = f32[40,128]{1,0:T(8,128)S(1)} copy-done((f32[40,128]{1,0:T(8,128)S(1)}, f32[40,128]{1,0:T(8,128)}, u32[]{:S(2)}) %copy-start.5) | copy-done | bytes 20504
  5.6 0.0 copy-start.6
  5.6 0.7 %copy-done.6 = f32[40,56]{1,0:T(8,128)S(1)} copy-done((f32[40,56]{1,0:T(8,128)S(1)}, f32[40,56]{1,0:T(8,128)}, u32[]{:S(2)}) %copy-start.6) | copy-done | bytes 8984
  6.4 27.5 %shard_map.109 = f32[3,48,384]{2,1,0:T(8,128)S(1)} custom-call(f32[147,1,512]{2,1,0:T(1,128)S(1)} %bitcast.7, f32[36,2,256]{2,1,0:T(2,128)S(1)} %bitcast.8, s32[1,256]{1,0:T(1,128)S(1)} %copy-done.9, s32[1,256]{1,0:T(1,128)S(1)} %bitcast.9, s32[2,1,384]{2,1,0:T(1,128)S(1)} %copy-done.8, f32[40,56]{1,0:T(8,128)S(1)} %copy-done.6, f32[56,40]{1,0:T(8,128)S(1)} %copy-done.4, ...), custom_call_target="tpu_custom_call" | custom-call | tf_op jit(solution)/shard_map/pallas_call | solution.py:417
  33.8 0.7 %copy.13 = f32[1,3,48,384]{3,2,1,0:T(8,128)} copy(f32[1,3,48,384]{3,2,1,0:T(8,128)S(1)} %bitcast.6) | data formatting | bytes 442368
Async XLA Ops:
  0.0 0.7 %copy-start.7 = (f32[16,128]{1,0:T(8,128)S(1)}, f32[16,128]{1,0:T(8,128)}, u32[]{:S(2)}) copy-start(f32[16,128]{1,0:T(8,128)} %constant.16.clone.fold_in) | copy-start | bytes 24580
  0.0 0.7 %copy-start.8 = (s32[2,1,384]{2,1,0:T(1,128)S(1)}, s32[2,1,384]{2,1,0:T(1,128)}, u32[]{:S(2)}) copy-start(s32[2,1,384]{2,1,0:T(1,128)} %lists.1) | copy-start | bytes 9220
  0.0 0.7 %copy-start.10 = (s32[1,256,1]{1,2,0:T(1,128)S(1)}, s32[1,256,1]{1,2,0:T(1,128)}, u32[]{:S(2)}) copy-start(s32[1,256,1]{1,2,0:T(1,128)} %param.14) | copy-start | bytes 3076
  0.0 0.7 %copy-start.9 = (s32[1,256]{1,0:T(1,128)S(1)}, s32[1,256]{1,0:T(1,128)}, u32[]{:S(2)}) copy-start(s32[1,256]{1,0:T(1,128)} %slaves.1) | copy-start | bytes 3076
  0.7 1.0 %copy-start = (f32[1,3,49,512]{3,0,2,1:T(1,128)S(1)}, f32[1,3,49,512]{3,0,2,1:T(1,128)}, u32[]{:S(2)}) copy-start(f32[1,3,49,512]{3,0,2,1:T(1,128)} %param.11) | copy-start | bytes 903172
  1.7 0.9 %copy-start.1 = (f32[1,2,36,256]{3,1,2,0:T(2,128)S(1)}, f32[1,2,36,256]{3,1,2,0:T(2,128)}, u32[]{:S(2)}) copy-start(f32[1,2,36,256]{3,1,2,0:T(2,128)} %param.12) | copy-start | bytes 221188
  2.6 0.8 %copy-start.2 = (f32[128,16]{1,0:T(8,128)S(1)}, f32[128,16]{1,0:T(8,128)}, u32[]{:S(2)}) copy-start(f32[128,16]{1,0:T(8,128)} %constant.15.clone.tile_in) | copy-start | bytes 24580
  3.4 0.7 %copy-start.3 = (f32[56,64]{1,0:T(8,128)S(1)}, f32[56,64]{1,0:T(8,128)}, u32[]{:S(2)}) copy-start(f32[56,64]{1,0:T(8,128)} %constant.17.clone.join) | copy-start | bytes 43012
  4.2 0.7 %copy-start.4 = (f32[56,40]{1,0:T(8,128)S(1)}, f32[56,40]{1,0:T(8,128)}, u32[]{:S(2)}) copy-start(f32[56,40]{1,0:T(8,128)} %constant.13.clone.spread_t) | copy-start | bytes 26884
  4.9 0.7 %copy-start.5 = (f32[40,128]{1,0:T(8,128)S(1)}, f32[40,128]{1,0:T(8,128)}, u32[]{:S(2)}) copy-start(f32[40,128]{1,0:T(8,128)} %constant.14.clone.quad) | copy-start | bytes 61444
  5.6 0.7 %copy-start.6 = (f32[40,56]{1,0:T(8,128)S(1)}, f32[40,56]{1,0:T(8,128)}, u32[]{:S(2)}) copy-start(f32[40,56]{1,0:T(8,128)} %constant.12.clone.spread) | copy-start | bytes 26884

commit v3 on v2

--- a/solution.py
+++ b/solution.py
@@ -68,15 +68,11 @@
     weights = np.array(GAUSS_WEIGHTS)
     quad = np.zeros((QPAD, LANES), np.float32)
     quad[:QUADS] = (weights[:, None] * weights[None, :]).reshape(QUADS, 1)
-    tile = np.zeros((LANES, 16), np.float32)
-    for copy in range(12):
-        for j in range(TAIL):
-            tile[copy * TAIL + j, j] = 1
-    join = np.zeros((6 * SX + 8, 8 * SX), np.float32)
-    for la in range(SX):
-        for k in range(7):
-            join[6 * la + k, 8 * la + k] = 1
-    return spread, spread.T.copy(), quad, tile, tile.T.copy(), join
+    table = np.zeros((QPAD + NPAD + QPAD, LANES), np.float32)
+    table[:QPAD, :NPAD] = spread
+    table[QPAD : QPAD + NPAD, :QPAD] = spread.T
+    table[QPAD + NPAD :] = quad
+    return table
 
 
 def two(x):
@@ -116,16 +112,19 @@
     return out
 
 
-def head_mask(shape, part):
-    lane = lax.broadcasted_iota(jnp.int32, shape, 1)
-    return (lane >= HEAD * part) & (lane < HEAD * (part + 1))
-
-
-def tail_mask(shape, part):
-    lane = lax.broadcasted_iota(jnp.int32, shape, 2)
-    row = lax.broadcasted_iota(jnp.int32, shape, 1)
-    start = TAIL * (4 * part + row // 2)
-    return (lane >= start) & (lane < start + TAIL)
+def iota(shape, axis):
+    return lax.broadcasted_iota(jnp.int32, shape, axis)
+
+
+def head_mask(part):
+    lane = iota((1, LANES), 1)
+    return jnp.where((lane >= HEAD * part) & (lane < HEAD * (part + 1)), 1.0, 0.0)
+
+
+def tail_mask(part):
+    lane = iota((1, 8, LANES), 2)
+    start = TAIL * (4 * part + iota((1, 8, LANES), 1) // 2)
+    return jnp.where((lane >= start) & (lane < start + TAIL), 1.0, 0.0)
 
 
 def pack(rows, hot, tile, send, tiles, parts):
@@ -144,10 +143,10 @@
         for part in range(min(3, parts - 3 * group)):
             at = (3 * group + part) * count
             block = gathered[at : at + count, :LANES]
-            block = jnp.where(head_mask(block.shape, part), block, 0.0)
+            block = block * head_mask(part)
             heads = block if heads is None else heads + block
             block = gathered[at : at + count, LANES:].reshape(tiles, 8, LANES)
-            block = jnp.where(tail_mask(block.shape, part), block, 0.0)
+            block = block * tail_mask(part)
             tails = block if tails is None else tails + block
         at = BLOCK * group
         send[:, at : at + 8, :] = heads.reshape(tiles, 8, LANES)
@@ -166,9 +165,7 @@
         eight = jnp.concatenate([pair] * 4, axis=1)
         for part in range(min(3, parts - 3 * group)):
             firsts.append(turned[part * HEAD : (part + 1) * HEAD])
-            lasts.append(
-                jnp.where(tail_mask(eight.shape, part), eight, 0.0).reshape(count, LANES)
-            )
+            lasts.append((eight * tail_mask(part)).reshape(count, LANES))
     last = jnp.concatenate(lasts, axis=0)
     high, low = two(last)
     return jnp.concatenate(
@@ -178,11 +175,12 @@
 
 def kernel(
     sizes,
-    surf, coords, slaves, owners, lists, spread, spread_t, quad, tile_in, fold_in, join,
+    surf_in, coords_in, slaves_in, owners_in, lists_in, table_in,
     out,
+    surf, coords, slaves, owners, lists, table,
     held, lb1, lb2, value, tract, nodes, force_rows, elements, strips, pads,
     send1, recv1, send2, recv2, row_out, col_out, row_in, col_in, corner_in,
-    ss1, rs1, ss2, rs2, hs, hr,
+    ss1, rs1, ss2, rs2, hs, hr, loads,
 ):
     wx, wy, parts, pairs, segs = sizes
     tiles = wx * wy
@@ -192,21 +190,43 @@
     next_x, next_y = lax.rem(gx + 1, wx), lax.rem(gy + 1, wy)
     back_x, back_y = lax.rem(gx + wx - 1, wx), lax.rem(gy + wy - 1, wy)
 
+    operands = (
+        (lists_in, lists), (surf_in, surf), (owners_in, owners),
+        (slaves_in, slaves), (table_in, table), (coords_in, coords),
+    )
+    reads = [
+        pltpu.make_async_copy(src, dst, loads.at[i]) for i, (src, dst) in enumerate(operands)
+    ]
+    for read in reads:
+        read.start()
+
+    def repeat(step):
+        if tiles <= 16:
+            for j in range(tiles):
+                step(j)
+        else:
+            lax.fori_loop(0, tiles, lambda j, carry: (step(j), carry)[1], 0)
+
     barrier = pltpu.get_barrier_semaphore()
 
-    def greet(j, carry):
+    def greet(j):
         to = lax.rem(here + j, tiles)
         pl.semaphore_signal(
             barrier, inc=1, device_id=(other, to // wy, lax.rem(to, wy)), device_id_type=MESH
         )
-        return carry
-
-    lax.fori_loop(0, tiles, greet, 0)
+
+    repeat(greet)
     for place in ((back_x, gy), (gx, back_y), (back_x, back_y)):
         pl.semaphore_signal(barrier, inc=1, device_id=(body,) + place, device_id_type=MESH)
 
-    tile = tile_in[...].astype(BF16)
-    fold = fold_in[...].astype(BF16)
+    row, step = iota((LANES, 16), 0), iota((LANES, 16), 1)
+    tile = flag((row - TAIL * (row // TAIL) == step) & (row < 12 * TAIL))
+    row, step = iota((16, LANES), 1), iota((16, LANES), 0)
+    fold = flag((row - TAIL * (row // TAIL) == step) & (row < 12 * TAIL))
+    row, step = iota((6 * SX + 8, 8 * SX), 0), iota((6 * SX + 8, 8 * SX), 1)
+    la = step // 8
+    together = flag((row == 6 * la + (step - 8 * la)) & (step - 8 * la < 7))
+    reads[0].wait()
 
     own = jnp.where(body == 0, lists[0], lists[1])
     pick = own.shape[1]
@@ -223,34 +243,24 @@
         return pltpu.make_async_remote_copy(
             src_ref=send.at[c, to],
             dst_ref=recv.at[c, land],
-            send_sem=ss.at[c, to],
-            recv_sem=rs.at[c, land],
+            send_sem=ss.at[c],
+            recv_sem=rs.at[c],
             device_id=(other, to // wy, lax.rem(to, wy)),
             device_id_type=MESH,
         )
 
     def start_all(*where):
-        def step(j, carry):
-            copy_of(*where, lax.rem(here + j, tiles), here).start()
-            return carry
-
-        lax.fori_loop(0, tiles, step, 0)
-
-    def wait_all(*where, arrive):
-        def step(j, carry):
-            copy = copy_of(*where, j, j)
-            if arrive:
-                copy.wait_recv()
-            else:
-                copy.wait_send()
-            return carry
-
-        lax.fori_loop(0, tiles, step, 0)
+        repeat(lambda j: copy_of(*where, lax.rem(here + j, tiles), here).start())
+
+    def wait_all(c, send, recv, ss, rs, arrive):
+        whole, sem = (recv, rs) if arrive else (send, ss)
+        pltpu.make_async_copy(whole.at[c], whole.at[c], sem.at[c]).wait()
 
     there = (send1, recv1, ss1, rs1)
     back = (send2, recv2, ss2, rs2)
 
     held[...] = jnp.zeros_like(held)
+    reads[1].wait()
     for c in range(3):
         held[c, :NODES, :] = surf[c * NODES : (c + 1) * NODES, 0, :]
         pack(held[c], list_hot, tile, send1.at[c], tiles, parts)
@@ -258,6 +268,8 @@
             pl.semaphore_wait(barrier, tiles + 3)
         start_all(c, *there)
 
+    for read in reads[2:]:
+        read.wait()
     tile_row = lax.broadcasted_iota(jnp.int32, (tiles, pairs), 0)
     same = flag(tile_row == owners[...])
     earlier = flag(
@@ -271,8 +283,8 @@
     slot_hot = flag(lax.broadcasted_iota(jnp.int32, (8 * tiles * parts, pairs), 0) == slot)
     slave_hot = flag(lax.broadcasted_iota(jnp.int32, (segs, pairs), 0) == slaves[...])
 
-    table_high, table_low = two(spread[...])
-    back_high, back_low = two(spread_t[...])
+    table_high, table_low = two(table[:QPAD, :NPAD])
+    back_high, back_low = two(table[QPAD : QPAD + NPAD, :QPAD])
     for c in range(3):
         high, low = two(held[c])
         high, low = two(dot(high, slave_hot) + dot(low, slave_hot))
@@ -292,7 +304,6 @@
     target = lax.broadcasted_iota(jnp.int32, (7 * SY, wide), 1)
     step_m = source // SY
     weave = flag(target == 6 * (source - step_m * SY) + step_m)
-    together = join[...].astype(BF16)
 
     pads[...] = jnp.zeros_like(pads)
     force_rows[...] = jnp.zeros_like(force_rows)
@@ -323,7 +334,7 @@
                     gap = -sign * offset
                     soft = jnp.maximum(gap, 0.0) + jnp.log1p(jnp.exp(-jnp.abs(gap)))
                     force = -sign * KAPPA * soft
-                tract[c, at, across] = force * quad[at, :]
+                tract[c, at, across] = force * table[QPAD + NPAD + 8 * chunk : QPAD + NPAD + 8 * chunk + 8, :]
         for across in blocks:
             minus = -tract[c, :, across]
             for m in range(7):
@@ -417,9 +428,15 @@
     result = pl.pallas_call(
         functools.partial(kernel, sizes),
         out_shape=jax.ShapeDtypeStruct((3, 6 * SX, 6 * SY), F32),
-        in_specs=[vmem] * 11,
+        in_specs=[pl.BlockSpec(memory_space=pl.ANY)] * 6,
         out_specs=vmem,
         scratch_shapes=[
+            pltpu.VMEM((3 * NODES, 1, segs), F32),
+            pltpu.VMEM((QUADS, 2, pairs), F32),
+            pltpu.VMEM((1, pairs), jnp.int32),
+            pltpu.VMEM((1, pairs), jnp.int32),
+            pltpu.VMEM((2, 1, tiles * slots), jnp.int32),
+            pltpu.VMEM((QPAD + NPAD + QPAD, LANES), F32),
             pltpu.VMEM((3, NPAD, segs), F32),
             pltpu.VMEM((7, QPAD, pairs), F32),
             pltpu.VMEM((7, QPAD, pairs), F32),
@@ -439,15 +456,16 @@
             pltpu.VMEM((3, 1, 6 * SY), F32),
             pltpu.VMEM((3, 1, 6 * SX + 8), F32),
             pltpu.VMEM((3, 1, 6 * SX + 8), F32),
-            pltpu.SemaphoreType.DMA((3, tiles)),
-            pltpu.SemaphoreType.DMA((3, tiles)),
-            pltpu.SemaphoreType.DMA((3, tiles)),
-            pltpu.SemaphoreType.DMA((3, tiles)),
+            pltpu.SemaphoreType.DMA((3,)),
+            pltpu.SemaphoreType.DMA((3,)),
+            pltpu.SemaphoreType.DMA((3,)),
+            pltpu.SemaphoreType.DMA((3,)),
             pltpu.SemaphoreType.DMA((3, 3)),
             pltpu.SemaphoreType.DMA((3, 3)),
+            pltpu.SemaphoreType.DMA((6,)),
         ],
         compiler_params=pltpu.CompilerParams(
-            collective_id=0, has_side_effects=True, vmem_limit_bytes=48 * 1024 * 1024
+            collective_id=0, has_side_effects=True, vmem_limit_bytes=60 * 1024 * 1024
         ),
     )(
         surface_disp.reshape(3 * NODES, 1, segs),
@@ -455,7 +473,7 @@
         pair_slave,
         pair_owner.reshape(1, pairs),
         lists,
-        *tables(),
+        tables(),
     )
     return result[None]
 

time: 35 us -> 28.5 us (0.81)
  local copies, waits for them, and re-layouts: 7.05 us -> 1.64 us
  Pallas kernels: 27.5 us -> 26.7 us
    unnamed x23 -> x1, local copies, waits for them, and re-layouts: 7.05 us -> 1.64 us
    pallas_call x1, Pallas kernels: 27.5 us -> 26.7 us  [local(): pl.pallas_call(functools.partial(kernel, sizes), out_shape=jax.ShapeDtype...]
where the time goes in v3:
time: 28.5 us; the launch traced here: 28.3 us
  Pallas kernels  26.7 us (94%)
  local copies, waits for them, and re-layouts  1.64 us (6%)
    pallas_call x1, Pallas kernels, local(): pl.pallas_call(functools.partial(kernel, sizes), out_shape=jax.ShapeDtype...  26.7 us
    unnamed x1, local copies, waits for them, and re-layouts  1.64 us

profile of v3, /device:TPU:0, one launch (start us, length us, event | category | flops | bytes accessed | tf_op | source)
XLA Modules:
  0.0 28.3 jit_solution(2121100232492770410)
XLA Ops:
  0.0 26.7 %shard_map.64 = f32[3,48,384]{2,1,0:T(8,128)} custom-call(f32[147,1,512]{2,1,0:T(1,128)} %bitcast.7, f32[36,2,256]{2,1,0:T(2,128)} %bitcast.8, s32[1,256]{1,0:T(1,128)} %slaves_in.1, s32[1,256]{1,0:T(1,128)} %bitcast.9, s32[2,1,384]{2,1,0:T(1,128)} %lists_in.1, f32[136,128]{1,0:T(8,128)} %constant.2.clone.table_in), custom_call_target="tpu_custom_call" | custom-call | tf_op jit(solution)/shard_map/pallas_call | solution.py:428
  26.7 1.6 %copy.8 = f32[1,3,48,384]{3,2,1,0:T(8,128)} copy(f32[1,3,48,384]{3,2,1,0:T(8,128)} %bitcast.6) | data formatting | bytes 442368

commit v4 on v3

--- a/solution.py
+++ b/solution.py
@@ -41,12 +41,14 @@
 F32 = jnp.float32
 BF16 = jnp.bfloat16
 NODES = 49
-NPAD = 56
+NPAD = 64
 LANES = 128
 HEAD = 40
 TAIL = NODES - HEAD
 QUADS = 36
 QPAD = 40
+QROWS = 48
+XPAD = 64
 BLOCK = 10
 SCALE = tuple(
     1.0 / float(np.prod([LOBATTO_POINTS[k] - LOBATTO_POINTS[m] for m in range(7) if m != k]))
@@ -68,10 +70,13 @@
     weights = np.array(GAUSS_WEIGHTS)
     quad = np.zeros((QPAD, LANES), np.float32)
     quad[:QUADS] = (weights[:, None] * weights[None, :]).reshape(QUADS, 1)
-    table = np.zeros((QPAD + NPAD + QPAD, LANES), np.float32)
-    table[:QPAD, :NPAD] = spread
-    table[QPAD : QPAD + NPAD, :QPAD] = spread.T
-    table[QPAD + NPAD :] = quad
+    high = spread.astype(BF16).astype(np.float32)
+    low = (spread - high).astype(BF16).astype(np.float32)
+    table = np.zeros((QPAD + NPAD + QPAD, 2 * LANES), np.float32)
+    for i, part in enumerate((high, high, low)):
+        table[:QPAD, i * NPAD : (i + 1) * NPAD] = part
+        table[QPAD : QPAD + NPAD, i * QROWS : i * QROWS + QPAD] = part.T
+    table[QPAD + NPAD :, :LANES] = quad
     return table
 
 
@@ -86,6 +91,18 @@
 
 def dot_t(a, b):
     return lax.dot_general(a, b, (((1,), (1,)), ((), ())), preferred_element_type=F32)
+
+
+def dot_parts(x, b):
+    rows = x.shape[0]
+    both = dot(jnp.concatenate(two(x), axis=0), b)
+    return both[:rows] + both[rows:]
+
+
+def dot_parts_t(x, b):
+    rows = x.shape[0]
+    both = dot_t(jnp.concatenate(two(x), axis=0), b)
+    return both[:rows] + both[rows:]
 
 
 def flag(condition):
@@ -132,11 +149,12 @@
     head = jnp.concatenate(
         [first, first, first, jnp.zeros((LANES - 3 * HEAD, first.shape[1]), F32)], axis=0
     )
-    gathered = None
-    for piece, tail in zip(two(head), two(rows[HEAD:])):
-        both = jnp.concatenate([piece, dot(tile, tail).astype(BF16)], axis=0)
-        term = dot_t(hot, both)
-        gathered = term if gathered is None else gathered + term
+    tails = jnp.concatenate(two(rows[HEAD : HEAD + 16]), axis=0)
+    tails = dot(tile, tails).astype(BF16)
+    high, low = two(head)
+    gathered = dot_t(hot, jnp.concatenate([high, tails[:LANES]], axis=0)) + dot_t(
+        hot, jnp.concatenate([low, tails[LANES:]], axis=0)
+    )
     count = 8 * tiles
     for group in range(-(-parts // 3)):
         heads, tails = None, None
@@ -167,9 +185,8 @@
             firsts.append(turned[part * HEAD : (part + 1) * HEAD])
             lasts.append((eight * tail_mask(part)).reshape(count, LANES))
     last = jnp.concatenate(lasts, axis=0)
-    high, low = two(last)
     return jnp.concatenate(
-        [jnp.concatenate(firsts, axis=1), dot_t(fold, high) + dot_t(fold, low)], axis=0
+        [jnp.concatenate(firsts, axis=1), dot_t(fold, jnp.concatenate(two(last), axis=1))], axis=0
     )
 
 
@@ -219,11 +236,16 @@
     for place in ((back_x, gy), (gx, back_y), (back_x, back_y)):
         pl.semaphore_signal(barrier, inc=1, device_id=(body,) + place, device_id_type=MESH)
 
-    row, step = iota((LANES, 16), 0), iota((LANES, 16), 1)
-    tile = flag((row - TAIL * (row // TAIL) == step) & (row < 12 * TAIL))
-    row, step = iota((16, LANES), 1), iota((16, LANES), 0)
-    fold = flag((row - TAIL * (row // TAIL) == step) & (row < 12 * TAIL))
-    row, step = iota((6 * SX + 8, 8 * SX), 0), iota((6 * SX + 8, 8 * SX), 1)
+    row, step = iota((2 * LANES, 32), 0), iota((2 * LANES, 32), 1)
+    place = row - LANES * (row // LANES)
+    copy = place // TAIL
+    tile = flag((place - TAIL * copy + 16 * (row // LANES) == step) & (copy < 12))
+    row, step = iota((24, 2 * LANES), 1), iota((24, 2 * LANES), 0)
+    place = row - LANES * (row // LANES)
+    copy = place // TAIL
+    fold = flag((place - TAIL * copy == step) & (copy < 12))
+    row, step = iota((XPAD, 16 * SX), 0), iota((XPAD, 16 * SX), 1)
+    step = step - 8 * SX * (step // (8 * SX))
     la = step // 8
     together = flag((row == 6 * la + (step - 8 * la)) & (step - 8 * la < 7))
     reads[0].wait()
@@ -250,7 +272,8 @@
         )
 
     def start_all(*where):
-        repeat(lambda j: copy_of(*where, lax.rem(here + j, tiles), here).start())
+        half = wy // 2 + tiles
+        repeat(lambda j: copy_of(*where, lax.rem(here + half - j, tiles), here).start())
 
     def wait_all(c, send, recv, ss, rs, arrive):
         whole, sem = (recv, rs) if arrive else (send, ss)
@@ -283,12 +306,10 @@
     slot_hot = flag(lax.broadcasted_iota(jnp.int32, (8 * tiles * parts, pairs), 0) == slot)
     slave_hot = flag(lax.broadcasted_iota(jnp.int32, (segs, pairs), 0) == slaves[...])
 
-    table_high, table_low = two(table[:QPAD, :NPAD])
-    back_high, back_low = two(table[QPAD : QPAD + NPAD, :QPAD])
-    for c in range(3):
-        high, low = two(held[c])
-        high, low = two(dot(high, slave_hot) + dot(low, slave_hot))
-        value[c] = dot(table_high, high) + (dot(table_high, low) + dot(table_low, high))
+    spread = table[:QPAD, : 3 * NPAD].astype(BF16)
+    for c in range(3):
+        high, low = two(dot_parts(held[c], slave_hot))
+        value[c] = dot(spread, jnp.concatenate([high, low, high], axis=0))
 
     for axis, store in ((0, lb1), (1, lb2)):
         place = jnp.concatenate(
@@ -299,12 +320,6 @@
             for k, factor in enumerate(basis(place[at])):
                 store[k, at, :] = factor
 
-    wide = SY * 6
-    source = lax.broadcasted_iota(jnp.int32, (7 * SY, wide), 0)
-    target = lax.broadcasted_iota(jnp.int32, (7 * SY, wide), 1)
-    step_m = source // SY
-    weave = flag(target == 6 * (source - step_m * SY) + step_m)
-
     pads[...] = jnp.zeros_like(pads)
     force_rows[...] = jnp.zeros_like(force_rows)
     sign = 1.0 - 2.0 * body.astype(F32)
@@ -312,12 +327,12 @@
 
     for c in range(3):
         wait_all(c, *there, arrive=True)
-        high, low = two(unpack(recv1.at[c], fold, tiles, parts))
-        nodes[...] = dot(high, slot_hot) + dot(low, slot_hot)
+        nodes[...] = dot_parts(unpack(recv1.at[c], fold, tiles, parts), slot_hot)
         for across in blocks:
             for chunk in range(QPAD // 8):
                 at = slice(8 * chunk, 8 * chunk + 8)
                 second = [lb2[k, at, across] for k in range(7)]
+                weight = table[QPAD + NPAD + 8 * chunk : QPAD + NPAD + 8 * chunk + 8, :LANES]
                 total = None
                 for k in range(7):
                     inner = None
@@ -334,7 +349,7 @@
                     gap = -sign * offset
                     soft = jnp.maximum(gap, 0.0) + jnp.log1p(jnp.exp(-jnp.abs(gap)))
                     force = -sign * KAPPA * soft
-                tract[c, at, across] = force * table[QPAD + NPAD + 8 * chunk : QPAD + NPAD + 8 * chunk + 8, :]
+                tract[c, at, across] = force * weight
         for across in blocks:
             minus = -tract[c, :, across]
             for m in range(7):
@@ -347,17 +362,23 @@
         pack(force_rows[...], slot_hot, tile, send2.at[c], tiles, parts)
         start_all(c, *back)
 
-    for c in range(3):
-        high, low = two(tract[c])
-        slave_force = dot(back_high, high) + (dot(back_high, low) + dot(back_low, high))
-        high, low = two(slave_force)
-        elements[c] = dot_t(high, slave_hot) + dot_t(low, slave_hot)
+    spread_t = table[QPAD : QPAD + NPAD, : 3 * QROWS].astype(BF16)
+    empty = jnp.zeros((QROWS - QPAD, pairs), F32)
+    for c in range(3):
+        high, low = two(jnp.concatenate([tract[c], empty], axis=0))
+        slave_force = dot(spread_t, jnp.concatenate([high, low, high], axis=0))
+        elements[c] = dot_parts_t(slave_force, slave_hot)
+
+    wide = SY * 6
+    source = lax.broadcasted_iota(jnp.int32, (7 * SY, wide), 0)
+    target = lax.broadcasted_iota(jnp.int32, (7 * SY, wide), 1)
+    step_m = source // SY
+    weave = flag(target == 6 * (source - step_m * SY) + step_m)
 
     halos = []
     for c in range(3):
         wait_all(c, *back, arrive=True)
-        high, low = two(unpack(recv2.at[c], fold, tiles, parts))
-        total = elements[c] + (dot(high, list_hot) + dot(low, list_hot))
+        total = elements[c] + dot_parts(unpack(recv2.at[c], fold, tiles, parts), list_hot)
         for block in range(segs // LANES):
             strips[block] = total[:, block * LANES : (block + 1) * LANES]
         for m in range(7):
@@ -365,11 +386,9 @@
                 block, lane = la * SY // LANES, la * SY % LANES
                 rows = strips[block, pl.ds(m, 8, stride=7), :]
                 pads[8 * la : 8 * la + 8, m * SY : (m + 1) * SY] = rows[:, lane : lane + SY]
-        high, low = two(pads[...])
-        joined = dot(together, high) + dot(together, low)
+        joined = dot(together, jnp.concatenate(two(pads[...]), axis=0))
         col_out[c] = joined[:, 7 * SY - LANES :].T[LANES - 1 :, :]
-        high, low = two(joined)
-        grid = dot(high, weave) + dot(low, weave)
+        grid = dot_parts(joined, weave)
         out[c] = grid[: 6 * SX]
         row_out[c] = grid[6 * SX : 6 * SX + 1]
         messages = [
@@ -397,11 +416,11 @@
         for copy in halos[3 * c : 3 * c + 3]:
             copy.wait_recv()
         corner = jnp.sum(
-            jnp.where(lanes[:, : 6 * SX + 8] == 6 * SX, corner_in[c], 0.0), axis=1, keepdims=True
+            jnp.where(lanes[:, :XPAD] == 6 * SX, corner_in[c], 0.0), axis=1, keepdims=True
         )
         row = row_in[c]
         out[c, 0:1, :] = out[c, 0:1, :] + row
-        edge = jnp.broadcast_to(col_in[c], (LANES, 6 * SX + 8)).T[: 6 * SX]
+        edge = jnp.broadcast_to(col_in[c], (LANES, XPAD)).T[: 6 * SX]
         first = (lax.broadcasted_iota(jnp.int32, edge.shape, 0) == 0).astype(F32)
         left = lax.broadcasted_iota(jnp.int32, edge.shape, 1) == 0
         out[c, :, :LANES] = out[c, :, :LANES] + jnp.where(left, edge + first * corner, 0.0)
@@ -436,7 +455,7 @@
             pltpu.VMEM((1, pairs), jnp.int32),
             pltpu.VMEM((1, pairs), jnp.int32),
             pltpu.VMEM((2, 1, tiles * slots), jnp.int32),
-            pltpu.VMEM((QPAD + NPAD + QPAD, LANES), F32),
+            pltpu.VMEM((QPAD + NPAD + QPAD, 2 * LANES), F32),
             pltpu.VMEM((3, NPAD, segs), F32),
             pltpu.VMEM((7, QPAD, pairs), F32),
             pltpu.VMEM((7, QPAD, pairs), F32),
@@ -452,10 +471,10 @@
             buffer,
             buffer,
             pltpu.VMEM((3, 1, 6 * SY), F32),
-            pltpu.VMEM((3, 1, 6 * SX + 8), F32),
+            pltpu.VMEM((3, 1, XPAD), F32),
             pltpu.VMEM((3, 1, 6 * SY), F32),
-            pltpu.VMEM((3, 1, 6 * SX + 8), F32),
-            pltpu.VMEM((3, 1, 6 * SX + 8), F32),
+            pltpu.VMEM((3, 1, XPAD), F32),
+            pltpu.VMEM((3, 1, XPAD), F32),
             pltpu.SemaphoreType.DMA((3,)),
             pltpu.SemaphoreType.DMA((3,)),
             pltpu.SemaphoreType.DMA((3,)),

time: 28.5 us -> 28.9 us (1.014)
  Pallas kernels: 26.7 us -> 27.1 us
    pallas_call x1, Pallas kernels: 26.7 us -> 27.1 us  [local(): pl.pallas_call(functools.partial(kernel, sizes), out_shape=jax.ShapeDtype...]
where the time goes in v4:
time: 28.9 us; the launch traced here: 28.8 us
  Pallas kernels  27.1 us (94%)
  local copies, waits for them, and re-layouts  1.64 us (6%)
    pallas_call x1, Pallas kernels, local(): pl.pallas_call(functools.partial(kernel, sizes), out_shape=jax.ShapeDtype...  27.1 us
    unnamed x1, local copies, waits for them, and re-layouts  1.64 us

profile of v4, /device:TPU:0, one launch (start us, length us, event | category | flops | bytes accessed | tf_op | source)
XLA Modules:
  0.0 28.8 jit_solution(2373565698145399824)
XLA Ops:
  0.0 27.1 %shard_map.64 = f32[3,48,384]{2,1,0:T(8,128)} custom-call(f32[147,1,512]{2,1,0:T(1,128)} %bitcast.7, f32[36,2,256]{2,1,0:T(2,128)} %bitcast.8, s32[1,256]{1,0:T(1,128)} %slaves_in.1, s32[1,256]{1,0:T(1,128)} %bitcast.9, s32[2,1,384]{2,1,0:T(1,128)} %lists_in.1, f32[144,256]{1,0:T(8,128)} %constant.2.clone.table_in), custom_call_target="tpu_custom_call" | custom-call | tf_op jit(solution)/shard_map/pallas_call | solution.py:447
  27.1 1.6 %copy.8 = f32[1,3,48,384]{3,2,1,0:T(8,128)} copy(f32[1,3,48,384]{3,2,1,0:T(8,128)} %bitcast.6) | data formatting | bytes 442368

commit v5 on v4

--- a/solution.py
+++ b/solution.py
@@ -144,7 +144,7 @@
     return jnp.where((lane >= start) & (lane < start + TAIL), 1.0, 0.0)
 
 
-def pack(rows, hot, tile, send, tiles, parts):
+def pack(rows, hot, tile, send, tiles, parts, ci, held):
     first = rows[:HEAD]
     head = jnp.concatenate(
         [first, first, first, jnp.zeros((LANES - 3 * HEAD, first.shape[1]), F32)], axis=0
@@ -166,20 +166,24 @@
             block = gathered[at : at + count, LANES:].reshape(tiles, 8, LANES)
             block = block * tail_mask(part)
             tails = block if tails is None else tails + block
-        at = BLOCK * group
-        send[:, at : at + 8, :] = heads.reshape(tiles, 8, LANES)
-        send[:, at + 8 : at + 10, :] = (tails[:, 0:2] + tails[:, 2:4]) + (
+        groups = -(-parts // 3)
+        at = ci * groups + group
+        send[:, 8 * at : 8 * at + 8, :] = heads.reshape(tiles, 8, LANES)
+        at = 8 * held * groups + 2 * at
+        send[:, at : at + 2, :] = (tails[:, 0:2] + tails[:, 2:4]) + (
             tails[:, 4:6] + tails[:, 6:8]
         )
 
 
-def unpack(recv, fold, tiles, parts):
+def unpack(recv, fold, tiles, parts, ci, held):
     count = 8 * tiles
     firsts, lasts = [], []
     for group in range(-(-parts // 3)):
-        at = BLOCK * group
-        turned = recv[:, at : at + 8, :].reshape(count, LANES).T
-        pair = recv[:, at + 8 : at + 10, :]
+        groups = -(-parts // 3)
+        at = ci * groups + group
+        turned = recv[:, 8 * at : 8 * at + 8, :].reshape(count, LANES).T
+        at = 8 * held * groups + 2 * at
+        pair = recv[:, at : at + 2, :]
         eight = jnp.concatenate([pair] * 4, axis=1)
         for part in range(min(3, parts - 3 * group)):
             firsts.append(turned[part * HEAD : (part + 1) * HEAD])
@@ -196,7 +200,7 @@
     out,
     surf, coords, slaves, owners, lists, table,
     held, lb1, lb2, value, tract, nodes, force_rows, elements, strips, pads,
-    send1, recv1, send2, recv2, row_out, col_out, row_in, col_in, corner_in,
+    send1a, send1b, recv1a, recv1b, send2a, send2b, recv2a, recv2b, row_out, col_out, row_in, col_in, corner_in,
     ss1, rs1, ss2, rs2, hs, hr, loads,
 ):
     wx, wy, parts, pairs, segs = sizes
@@ -263,8 +267,8 @@
 
     def copy_of(c, send, recv, ss, rs, to, land):
         return pltpu.make_async_remote_copy(
-            src_ref=send.at[c, to],
-            dst_ref=recv.at[c, land],
+            src_ref=send[c].at[to],
+            dst_ref=recv[c].at[land],
             send_sem=ss.at[c],
             recv_sem=rs.at[c],
             device_id=(other, to // wy, lax.rem(to, wy)),
@@ -277,19 +281,22 @@
 
     def wait_all(c, send, recv, ss, rs, arrive):
         whole, sem = (recv, rs) if arrive else (send, ss)
-        pltpu.make_async_copy(whole.at[c], whole.at[c], sem.at[c]).wait()
-
-    there = (send1, recv1, ss1, rs1)
-    back = (send2, recv2, ss2, rs2)
+        pltpu.make_async_copy(whole[c], whole[c], sem.at[c]).wait()
+
+    there = ((send1a, send1b), (recv1a, recv1b), ss1, rs1)
+    back = ((send2a, send2b), (recv2a, recv2b), ss2, rs2)
+    stages = ((0, 0, 2), (0, 1, 2), (1, 0, 1))
 
     held[...] = jnp.zeros_like(held)
     reads[1].wait()
     for c in range(3):
         held[c, :NODES, :] = surf[c * NODES : (c + 1) * NODES, 0, :]
-        pack(held[c], list_hot, tile, send1.at[c], tiles, parts)
-        if c == 0:
-            pl.semaphore_wait(barrier, tiles + 3)
-        start_all(c, *there)
+        stage, ci, count = stages[c]
+        pack(held[c], list_hot, tile, there[0][stage], tiles, parts, ci, count)
+        if ci == count - 1:
+            if stage == 0:
+                pl.semaphore_wait(barrier, tiles + 3)
+            start_all(stage, *there)
 
     for read in reads[2:]:
         read.wait()
@@ -326,8 +333,12 @@
     blocks = [slice(b * LANES, (b + 1) * LANES) for b in range(pairs // LANES)]
 
     for c in range(3):
-        wait_all(c, *there, arrive=True)
-        nodes[...] = dot_parts(unpack(recv1.at[c], fold, tiles, parts), slot_hot)
+        stage, ci, count = stages[c]
+        if ci == 0:
+            wait_all(stage, *there, arrive=True)
+        nodes[...] = dot_parts(
+            unpack(there[1][stage], fold, tiles, parts, ci, count), slot_hot
+        )
         for across in blocks:
             for chunk in range(QPAD // 8):
                 at = slice(8 * chunk, 8 * chunk + 8)
@@ -359,8 +370,9 @@
                     force_rows[row : row + 1, across] = jnp.sum(
                         lb1[k, :, across] * weighted, axis=0, keepdims=True
                     )
-        pack(force_rows[...], slot_hot, tile, send2.at[c], tiles, parts)
-        start_all(c, *back)
+        pack(force_rows[...], slot_hot, tile, back[0][stage], tiles, parts, ci, count)
+        if ci == count - 1:
+            start_all(stage, *back)
 
     spread_t = table[QPAD : QPAD + NPAD, : 3 * QROWS].astype(BF16)
     empty = jnp.zeros((QROWS - QPAD, pairs), F32)
@@ -377,8 +389,12 @@
 
     halos = []
     for c in range(3):
-        wait_all(c, *back, arrive=True)
-        total = elements[c] + dot_parts(unpack(recv2.at[c], fold, tiles, parts), list_hot)
+        stage, ci, count = stages[c]
+        if ci == 0:
+            wait_all(stage, *back, arrive=True)
+        total = elements[c] + dot_parts(
+            unpack(back[1][stage], fold, tiles, parts, ci, count), list_hot
+        )
         for block in range(segs // LANES):
             strips[block] = total[:, block * LANES : (block + 1) * LANES]
         for m in range(7):
@@ -408,9 +424,9 @@
             copy.start()
             halos.append(copy)
 
-    for c in range(3):
-        wait_all(c, *there, arrive=False)
-        wait_all(c, *back, arrive=False)
+    for stage in range(2):
+        wait_all(stage, *there, arrive=False)
+        wait_all(stage, *back, arrive=False)
     lanes = lax.broadcasted_iota(jnp.int32, (1, LANES), 1)
     for c in range(3):
         for copy in halos[3 * c : 3 * c + 3]:
@@ -443,7 +459,8 @@
         lists = lists.reshape(2, 1, tiles * slots)
     sizes = (wx, wy, parts, pairs, segs)
     vmem = pl.BlockSpec(memory_space=pltpu.VMEM)
-    buffer = pltpu.VMEM((3, tiles, BLOCK * -(-parts // 3), LANES), F32)
+    rows = BLOCK * -(-parts // 3)
+    buffers = [pltpu.VMEM((tiles, count * rows, LANES), F32) for count in (2, 1)]
     result = pl.pallas_call(
         functools.partial(kernel, sizes),
         out_shape=jax.ShapeDtypeStruct((3, 6 * SX, 6 * SY), F32),
@@ -466,19 +483,16 @@
             pltpu.VMEM((3, NPAD, segs), F32),
             pltpu.VMEM((segs // LANES, NPAD, LANES), F32),
             pltpu.VMEM((8 * SX, 7 * SY), F32),
-            buffer,
-            buffer,
-            buffer,
-            buffer,
+            *(buffers * 4),
             pltpu.VMEM((3, 1, 6 * SY), F32),
             pltpu.VMEM((3, 1, XPAD), F32),
             pltpu.VMEM((3, 1, 6 * SY), F32),
             pltpu.VMEM((3, 1, XPAD), F32),
             pltpu.VMEM((3, 1, XPAD), F32),
-            pltpu.SemaphoreType.DMA((3,)),
-            pltpu.SemaphoreType.DMA((3,)),
-            pltpu.SemaphoreType.DMA((3,)),
-            pltpu.SemaphoreType.DMA((3,)),
+            pltpu.SemaphoreType.DMA((2,)),
+            pltpu.SemaphoreType.DMA((2,)),
+            pltpu.SemaphoreType.DMA((2,)),
+            pltpu.SemaphoreType.DMA((2,)),
             pltpu.SemaphoreType.DMA((3, 3)),
             pltpu.SemaphoreType.DMA((3, 3)),
             pltpu.SemaphoreType.DMA((6,)),

time: 28.9 us -> 31.7 us (1.097)
  Pallas kernels: 27.1 us -> 29.9 us
    pallas_call x1, Pallas kernels: 27.1 us -> 29.9 us  [local(): pl.pallas_call(functools.partial(kernel, sizes), out_shape=jax.ShapeDtype...]
where the time goes in v5:
time: 31.7 us; the launch traced here: 31.5 us
  Pallas kernels  29.9 us (94%)
  local copies, waits for them, and re-layouts  1.64 us (5%)
    pallas_call x1, Pallas kernels, local(): pl.pallas_call(functools.partial(kernel, sizes), out_shape=jax.ShapeDtype...  29.9 us
    unnamed x1, local copies, waits for them, and re-layouts  1.64 us

profile of v5, /device:TPU:0, one launch (start us, length us, event | category | flops | bytes accessed | tf_op | source)
XLA Modules:
  0.0 31.5 jit_solution(8161792718168398340)
XLA Ops:
  0.0 29.9 %shard_map.64 = f32[3,48,384]{2,1,0:T(8,128)} custom-call(f32[147,1,512]{2,1,0:T(1,128)} %bitcast.7, f32[36,2,256]{2,1,0:T(2,128)} %bitcast.8, s32[1,256]{1,0:T(1,128)} %slaves_in.1, s32[1,256]{1,0:T(1,128)} %bitcast.9, s32[2,1,384]{2,1,0:T(1,128)} %lists_in.1, f32[144,256]{1,0:T(8,128)} %constant.2.clone.table_in), custom_call_target="tpu_custom_call" | custom-call | tf_op jit(solution)/shard_map/pallas_call | solution.py:464
  29.9 1.6 %copy.8 = f32[1,3,48,384]{3,2,1,0:T(8,128)} copy(f32[1,3,48,384]{3,2,1,0:T(8,128)} %bitcast.6) | data formatting | bytes 442368
